TPU v7x, 256 devices: a whole 4x4x8 slice. The times are simulated.
256 devices in a mesh: dp: 64 (over x, z, core), tensor: 4 (over y).
Axes of the slice: x: 4, y: 4, z: 8, core: 2. Of those that a mesh axis runs over, the one named last changes fastest.
Arguments:
- cotangent: bfloat16 [16384, 4096], P(('dp', 'tensor')), may hold values from -6 to 6
- gate_pre: bfloat16 [16384, 1024], P('dp', 'tensor'), may hold values from -6 to 6
- up_pre: bfloat16 [16384, 1024], P('dp', 'tensor'), may hold values from -6 to 6
- down_weight: bfloat16 [1024, 4096], P('tensor'), may hold values from -0.1875 to 0.1875
- gate_weight: bfloat16 [4096, 1024], P(None, 'tensor'), may hold values from -0.09375 to 0.09375
- up_weight: bfloat16 [4096, 1024], P(None, 'tensor'), may hold values from -0.09375 to 0.09375
- error_in: bfloat16 [64, 1024, 4096], P('dp', 'tensor'), may hold values from -6 to 6
- factor_in: float32 [4, 64, 4096], P('tensor'), may hold values from -6 to 6
Outputs:
- input_grad: bfloat16 [16384, 4096], P(('dp', 'tensor'))
- left_out: float32 [1024, 64], P('tensor')
- right_mean: float32 [4, 64, 4096], P('tensor')
- error_out: bfloat16 [64, 1024, 4096], P('dp', 'tensor')
All inputs are finite; a program needn't handle non-finite values.
Results may differ from a plain program's by a relative error of at most 0.013.
Values may be sent and summed in bfloat16 or wider, within the bound.
A program may use at most 64 MiB of HBM per device.

v0:
```python
import jax
import jax.numpy as jnp
from jax import lax
from jax.sharding import PartitionSpec as P

epsilon = 1e-06


def swiglu_back(grad_hidden, gate_pre, up_pre):
    gate_values = gate_pre.astype(jnp.float32)
    up_values = up_pre.astype(jnp.float32)
    sigmoid_gate = jax.nn.sigmoid(gate_values)
    silu_gate = gate_values * sigmoid_gate
    hidden = (silu_gate * up_values).astype(jnp.bfloat16)
    d_gate = (
        grad_hidden * up_values * sigmoid_gate * (1.0 + gate_values * (1.0 - sigmoid_gate))
    ).astype(jnp.bfloat16)
    d_up = (grad_hidden * silu_gate).astype(jnp.bfloat16)
    return (hidden, d_gate, d_up)


def orthonormal(matrix):
    count_rows = matrix.shape[0]

    def step(column, current_tile):
        vector = lax.dynamic_index_in_dim(current_tile, column, 0, keepdims=False)
        vector = vector / jnp.sqrt(jnp.sum(vector * vector) + epsilon)
        correlation = jnp.dot(current_tile, vector, precision=lax.Precision.HIGHEST)
        later_rows = jnp.arange(count_rows) > column
        current_tile = (
            current_tile
            - jnp.where(later_rows, correlation, jnp.zeros_like(correlation))[:, None]
            * vector[None, :]
        )
        return lax.dynamic_update_index_in_dim(current_tile, vector, column, 0)

    return lax.fori_loop(0, count_rows, step, matrix)


def transposed_product(left_side, right_side):
    return lax.dot_general(
        left_side, right_side, (((1,), (1,)), ((), ())), preferred_element_type=jnp.float32
    )


def shards(cotangent, gate_pre, up_pre, down_weight, gate_weight, up_weight, error_in, factor_in):
    replicas = lax.axis_size("dp")
    local_rows = cotangent.shape[0]
    gathered = lax.all_gather(cotangent, "tensor", axis=0, tiled=True)
    grad_hidden = transposed_product(gathered, down_weight)
    hidden, d_gate, d_up = swiglu_back(grad_hidden, gate_pre, up_pre)
    summed = lax.psum(
        (transposed_product(d_gate, gate_weight) + transposed_product(d_up, up_weight)).astype(
            jnp.bfloat16
        ),
        "tensor",
    ).astype(jnp.float32)
    own_rows = lax.dynamic_slice_in_dim(
        summed, lax.axis_index("tensor") * local_rows, local_rows, 0
    )
    input_grad = own_rows.astype(jnp.bfloat16)
    weight_grad = lax.dot_general(
        hidden, gathered, (((0,), (0,)), ((), ())), preferred_element_type=jnp.float32
    )
    weight_grad = weight_grad + error_in[0].astype(jnp.float32)
    left_local = lax.dot_general(
        weight_grad, factor_in[0], (((1,), (1,)), ((), ())), precision=lax.Precision.HIGHEST
    )
    left_sum = lax.psum(left_local, "dp") / replicas
    orthonormal_rows = orthonormal(left_sum.T)
    right_partial = jnp.dot(orthonormal_rows, weight_grad, precision=lax.Precision.HIGHEST)
    right_sum = lax.psum(right_partial, "dp") / replicas
    approximation = lax.dot_general(
        orthonormal_rows, right_sum, (((0,), (0,)), ((), ())), precision=lax.Precision.HIGHEST
    )
    error_out = (weight_grad - approximation).astype(jnp.bfloat16)
    return (input_grad, orthonormal_rows.T, right_sum[None], error_out[None])


def solution(mesh):
    in_specs = (
        P(("dp", "tensor"), None),
        P("dp", "tensor"),
        P("dp", "tensor"),
        P("tensor", None),
        P(None, "tensor"),
        P(None, "tensor"),
        P("dp", "tensor", None),
        P("tensor", None, None),
    )
    out_specs = (
        P(("dp", "tensor"), None),
        P("tensor", None),
        P("tensor", None, None),
        P("dp", "tensor", None),
    )
    return jax.shard_map(shards, mesh=mesh, in_specs=in_specs, out_specs=out_specs, check_vma=False)
```

profile of v0, /device:TPU:1, one launch (start us, length us, event | category | flops | bytes accessed | tf_op | source)
XLA Modules:
  0.0 591.3 jit_solution(15156226357853846531)
XLA Ops:
  7.2 0.7 all-gather.2.cloned.1.call-update
  8.0 39.1 %all-gather.2.cloned.1.call-done = bf16[256,4096]{1,0:T(8,128)(2,1)} async-done(((bf16[64,4096]{1,0:T(8,128)(2,1)}), bf16[256,4096]{1,0:T(8,128)(2,1)}) %all-gather.2.cloned.1.call-update) | async-done | bytes 2097168 | tf_op jit(solution)/shard_map/all_gather | solution.py:49
  47.1 3.2 convolution_add_fusion
  50.2 1.9 copy-done.1
  52.2 4.6 fusion.5
  56.8 3.0 fusion.25
  59.8 165.1 %all-reduce.6.cloned.1.call-done = f32[256,64]{0,1:T(8,128)} async-done(((f32[256,64]{0,1:T(8,128)}), f32[256,64]{0,1:T(8,128)}) %all-reduce.6.cloned.1.call-update) | async-done | bytes 65552 | tf_op jit(solution)/shard_map/psum | solution.py:69
  224.9 0.8 multiply_bitcast_fusion.1
  225.8 105.2 %while.13 = (s32[]{:T(128)}, f32[64,256]{1,0:T(8,128)S(1)}, s32[]{:T(128)}, f32[]{:T(128)}, s32[]{:T(128)}) while((s32[]{:T(128)}, f32[64,256]{1,0:T(8,128)S(1)}, s32[]{:T(128)}, f32[]{:T(128)}, s32[]{:T(128)}) %tuple.32), condition=%wide.region_4.5_spmd, body=%wide.region_2.4_spmd.sunk | while | flops 230274 | bytes 204401 | solution.py:37
  227.4 0.6 multiply_reduce_fusion.2
  229.1 0.6 multiply_reduce_fusion.2
  230.7 0.6 multiply_reduce_fusion.2
  232.4 0.6 multiply_reduce_fusion.2
  234.0 0.6 multiply_reduce_fusion.2
  235.6 0.6 multiply_reduce_fusion.2
  238.9 0.6 multiply_reduce_fusion.2
  242.2 0.6 multiply_reduce_fusion.2
  245.5 0.6 multiply_reduce_fusion.2
  248.8 0.6 multiply_reduce_fusion.2
  252.1 0.6 multiply_reduce_fusion.2
  253.7 0.6 multiply_reduce_fusion.2
  255.4 0.6 multiply_reduce_fusion.2
  257.0 0.6 multiply_reduce_fusion.2
  258.7 0.6 multiply_reduce_fusion.2
  260.3 0.6 multiply_reduce_fusion.2
  261.9 0.6 multiply_reduce_fusion.2
  263.6 0.6 multiply_reduce_fusion.2
  265.2 0.6 multiply_reduce_fusion.2
  266.9 0.6 multiply_reduce_fusion.2
  270.2 0.6 multiply_reduce_fusion.2
  273.5 0.6 multiply_reduce_fusion.2
  276.7 0.6 multiply_reduce_fusion.2
  280.0 0.6 multiply_reduce_fusion.2
  283.3 0.6 multiply_reduce_fusion.2
  285.0 0.6 multiply_reduce_fusion.2
  286.6 0.6 multiply_reduce_fusion.2
  288.3 0.6 multiply_reduce_fusion.2
  289.9 0.6 multiply_reduce_fusion.2
  291.5 0.6 multiply_reduce_fusion.2
  293.2 0.6 multiply_reduce_fusion.2
  294.8 0.6 multiply_reduce_fusion.2
  296.5 0.6 multiply_reduce_fusion.2
  298.1 0.6 multiply_reduce_fusion.2
  301.4 0.6 multiply_reduce_fusion.2
  304.7 0.6 multiply_reduce_fusion.2
  308.0 0.6 multiply_reduce_fusion.2
  311.3 0.6 multiply_reduce_fusion.2
  314.6 0.6 multiply_reduce_fusion.2
  316.2 0.6 multiply_reduce_fusion.2
  317.9 0.6 multiply_reduce_fusion.2
  319.5 0.6 multiply_reduce_fusion.2
  321.1 0.6 multiply_reduce_fusion.2
  322.8 0.6 multiply_reduce_fusion.2
  324.4 0.6 multiply_reduce_fusion.2
  326.1 0.6 multiply_reduce_fusion.2
  331.0 5.8 fusion.26
  337.0 0.8 fusion.18
  337.8 0.8 copy-done.4
  338.6 2.1 fusion.3
  340.7 176.9 %all-reduce.8.cloned.1.call-done = f32[64,4096]{1,0:T(8,128)} async-done(((f32[64,4096]{1,0:T(8,128)}), f32[64,4096]{1,0:T(8,128)}) %all-reduce.8.cloned.1.call-update) | async-done | bytes 1048592 | tf_op jit(solution)/shard_map/psum | solution.py:72
  517.6 7.0 %fusion.4 = bf16[1,256,4096]{2,1,0:T(8,128)(2,1)} fusion(f32[256,4096]{1,0:T(8,128)} %copy-done.1, f32[64,256]{1,0:T(8,128)S(1)} %get-tuple-element.53, f32[64,4096]{1,0:T(8,128)} %all-reduce.8.cloned.1.call-done), kind=kOutput, calls=%fused_computation.11 | convolution fusion | flops 807665664 | bytes 7405568 | tf_op jit(solution)/shard_map/dot_general | solution.py:73
  524.5 1.1 multiply_bitcast_fusion
  525.6 57.3 %all-reduce.4.cloned.1.call-done = bf16[256,4096]{1,0:T(8,128)(2,1)} async-done(((bf16[256,4096]{1,0:T(8,128)(2,1)}), bf16[256,4096]{1,0:T(8,128)(2,1)}) %all-reduce.4.cloned.1.call-update) | async-done | bytes 2097168 | tf_op jit(solution)/shard_map/psum | solution.py:52
  582.9 1.9 convert_convert_fusion
  (295 shorter events, 30.8 us)
Async XLA Ops:
  7.2 329.8 %copy-start = (bf16[4096,256]{1,0:T(8,128)(2,1)S(1)}, bf16[4096,256]{1,0:T(8,128)(2,1)}, u32[]{:S(2)}) copy-start(bf16[4096,256]{1,0:T(8,128)(2,1)} %param.14) | copy-start | bytes 6291460
  7.2 39.9 %all-gather.2.cloned.1.call-start = ((), (), s32[]{:S(2)}) async-start(), calls=%async_computation | async-start | bytes 2621440 | tf_op jit(solution)/shard_map/all_gather | solution.py:49
  7.9 217.0 %all-reduce.6.cloned.1.call-start = ((), (), s32[]{:S(2)}) async-start(), calls=%async_computation.2 | async-start | bytes 131072 | tf_op jit(solution)/shard_map/psum | solution.py:69
  8.0 44.2 %copy-start.6 = (f32[1,64,4096]{2,1,0:T(8,128)S(1)}, f32[1,64,4096]{2,1,0:T(8,128)}, u32[]{:S(2)}) copy-start(f32[1,64,4096]{2,1,0:T(8,128)} %param.17) | copy-start | bytes 3145732
  50.2 1.9 copy-start.1
  56.8 460.8 %all-reduce.8.cloned.1.call-start = ((), (), s32[]{:S(2)}) async-start(), calls=%async_computation.3 | async-start | bytes 2097152 | tf_op jit(solution)/shard_map/psum | solution.py:72
  331.0 186.6 %copy-start.2 = (f32[64,256]{1,0:T(8,128)}, f32[64,256]{1,0:T(8,128)S(1)}, u32[]{:S(2)}) copy-start(f32[64,256]{1,0:T(8,128)S(1)} %get-tuple-element.53) | copy-start | bytes 196612
  331.0 5.9 %copy-start.5 = (bf16[256,256]{1,0:T(8,128)(2,1)S(1)}, bf16[256,256]{1,0:T(8,128)(2,1)}, u32[]{:S(2)}) copy-start(bf16[256,256]{1,0:T(8,128)(2,1)} %param.11) | copy-start | bytes 393220
  331.0 5.9 %copy-start.7 = (bf16[256,256]{1,0:T(8,128)(2,1)S(1)}, bf16[256,256]{1,0:T(8,128)(2,1)}, u32[]{:S(2)}) copy-start(bf16[256,256]{1,0:T(8,128)(2,1)} %param.12) | copy-start | bytes 393220
  336.9 246.0 %all-reduce.4.cloned.1.call-start = ((), (), s32[]{:S(2)}) async-start(), calls=%async_computation.1 | async-start | bytes 4194304 | tf_op jit(solution)/shard_map/psum | solution.py:52
  337.0 1.6 copy-start.4
  517.6 7.0 %copy-start.3 = (f32[64,4096]{1,0:T(8,128)S(1)}, f32[64,4096]{1,0:T(8,128)}, u32[]{:S(2)}) copy-start(f32[64,4096]{1,0:T(8,128)} %all-reduce.8.cloned.1.call-done) | copy-start | bytes 3145732
Sparse Core Ops, SparseCore 0:
  9.8 37.2 all-gather.1
  56.9 167.9 all-reduce.5
  337.0 180.4 all-reduce.7
  519.9 62.9 all-reduce.3
where the time goes:
time: 593 us; the launch traced here: 591 us
  waiting for transfers between devices  439 us (74%)
  other arithmetic  50.7 us (9%)
  loops' own time  46.7 us (8%)
  matrix products  35.3 us (6%)
  between operations  13.9 us (2%)
    psum x1, waiting for transfers between devices, shards(): right_sum = lax.psum(right_partial, 'dp') / replicas  177 us
    psum x1, waiting for transfers between devices, shards(): left_sum = lax.psum(left_local, 'dp') / replicas  165 us
    psum x1, waiting for transfers between devices, shards(): lax.psum((transposed_product(d_gate, gate_weight) + transposed_product(d_...  57.3 us
    another operation x1, loops' own time, orthonormal(): return lax.fori_loop(0, count_rows, step, matrix)  46.7 us
    all_gather x1, waiting for transfers between devices, shards(): gathered = lax.all_gather(cotangent, 'tensor', axis=0, tiled=True)  39.1 us
    reduce_sum x64, other arithmetic, step(): vector = vector / jnp.sqrt(jnp.sum(vector * vector) + epsilon)  38.9 us
  transfers between devices with their start and end apart: 4, of which 4 were waited for; matrix products, arithmetic and copies ran while one was open for 2% of the time, Pallas kernels for 0%

commit v1 on v0

v1 whole, which is shorter than its diff:
```python
import functools

import jax
import jax.numpy as jnp
from jax import lax
from jax.experimental import pallas as pl
from jax.experimental.pallas import tpu as pltpu
from jax.sharding import PartitionSpec as P

epsilon = 1e-06
NX, NZ, NC = 4, 8, 2
NY = 4
MESH = pl.DeviceIdType.MESH
f32, bf16 = jnp.float32, jnp.bfloat16
NN = (((1,), (0,)), ((), ()))
NT = (((1,), (1,)), ((), ()))


def dot(a, b, dims=NN):
    return lax.dot_general(a, b, dims, preferred_element_type=f32)


def split(a):
    high = a.astype(bf16)
    low = (a - high.astype(f32)).astype(bf16)
    return jnp.concatenate([high, low], axis=0)


def fold(a):
    half = a.shape[0] // 2
    return a[:half] + a[half:]


def kernel(
    c, gate, up, wd, wg, wu, e, f,
    ig, left_out, right_out, err,
    cbuf, wd_v, wg_v, wu_v, e_v, f_v, fs, gate_v, up_v, hid, hid_t, y_v, pe, dg, du,
    part, ig_in, ig_sum, ig_v,
    p1, p1_in, p2_in, t_v, ts, tt, zs, m_v,
    r1, r1_in, r2, r2_in, r3, r4_in, right_v, err_v,
    load, ag_s, ag_r, p1_s, p1_r, p2_s, p2_r, p3_s, p3_r,
    r1_s, r1_r, r2_s, r2_r, r3_s, r3_r, r4_s, r4_r, ig_s, ig_r, out_s,
):
    G = NX * NC
    rows, D = c.shape
    half = rows // 2
    TOK = NY * rows
    F = wd.shape[0]
    RANK = f.shape[0]
    prow = RANK // G
    HC = G // 4
    zw = D // HC // NZ
    width = 512 if D >= 4096 else 256

    dp, y = lax.axis_index("dp"), lax.axis_index("tensor")
    core = lax.rem(dp, NC)
    z = lax.rem(dp // NC, NZ)
    x = dp // (NC * NZ)
    g = x * NC + core
    y_right, y_left, y_opp = (lax.rem(y + k, NY) for k in (1, 3, 2))

    def in_group(d):
        other = lax.rem(g + d, G)
        return (((other // NC) * NZ + z) * NC + lax.rem(other, NC), y)

    def in_z(d):
        return ((x * NZ + lax.rem(z + d, NZ)) * NC + core, y)

    mine = cbuf.at[y]
    pairs = [(c, mine), (f, f_v), (e, e_v), (gate, gate_v), (up, up_v), (wd, wd_v), (wg, wg_v), (wu, wu_v)]
    loads = [pltpu.make_async_copy(a, b, load.at[k]) for k, (a, b) in enumerate(pairs)]
    for copy in loads:
        copy.start()

    barrier = pltpu.get_barrier_semaphore()
    partners = [(dp, y_right), (dp, y_left)]
    partners += [in_group(d) for d in range(1, G)] + [in_z(d) for d in range(1, NZ)]
    for other in partners:
        pl.semaphore_signal(barrier, inc=1, device_id=other, device_id_type=MESH)
    pl.semaphore_wait(barrier, len(partners))

    def send(src, dst, s, r, to):
        copy = pltpu.make_async_remote_copy(
            src_ref=src, dst_ref=dst, send_sem=s, recv_sem=r, device_id=to, device_id_type=MESH
        )
        copy.start()
        return copy

    sent = []
    right, left = (dp, y_right), (dp, y_left)
    A, B = pl.ds(0, half), pl.ds(half, half)

    def gather(k, src, dst, to):
        copy = send(src, dst, ag_s.at[k], ag_r.at[k], to)
        sent.append(copy)
        return copy

    from_left_a = gather(0, c.at[A], cbuf.at[y, A], right)
    from_right_b = gather(1, c.at[B], cbuf.at[y, B], left)
    from_left_b = gather(2, c.at[B], cbuf.at[y, B], right)
    from_right_a = gather(3, c.at[A], cbuf.at[y, A], left)

    loads[1].wait()
    fs[...] = split(f_v[...])
    loads[0].wait()

    def tokens_times_factor(slot):
        both = dot(cbuf[slot], fs[...], NT)
        y_v[slot] = both[:, :RANK] + both[:, RANK:]

    tokens_times_factor(y)
    loads[2].wait()
    pe[...] = fold(dot(fs[...], e_v[...], NT))
    loads[3].wait()
    loads[4].wait()
    a, u = gate_v[...].astype(f32), up_v[...].astype(f32)
    hidden = a * jax.nn.sigmoid(a) * u
    hidden = hidden.astype(bf16).astype(f32)
    hid[...] = hidden.astype(bf16)
    hid_t[...] = hidden.T.astype(bf16)

    from_left_a.wait_recv()
    from_opp_a = gather(4, cbuf.at[y_left, A], cbuf.at[y_left, A], right)
    from_right_b.wait_recv()
    from_opp_b = gather(5, cbuf.at[y_right, B], cbuf.at[y_right, B], left)
    from_left_b.wait_recv()
    tokens_times_factor(y_left)
    from_right_a.wait_recv()
    tokens_times_factor(y_right)
    from_opp_a.wait_recv()
    from_opp_b.wait_recv()
    tokens_times_factor(y_opp)

    y_all = y_v[...].reshape(TOK, RANK)
    y_high = y_all.astype(bf16).astype(f32)
    y_both = jnp.concatenate([y_high, y_all - y_high], axis=1).T.astype(bf16)
    p_all = fold(dot(y_both, hid[...])) + pe[...]
    p1[...] = p_all.reshape(G, prow, F)

    p1_copies = []
    for d in range(1, G):
        other = lax.rem(g + d, G)
        p1_copies.append(send(p1.at[other], p1_in.at[g], p1_s.at[d], p1_r.at[d], in_group(d)))
    p1_in[g] = p1[g]

    loads[5].wait()
    grad = dot(cbuf[...].reshape(TOK, D), wd_v[...], NT)
    a, u = gate_v[...].astype(f32), up_v[...].astype(f32)
    s = jax.nn.sigmoid(a)
    dg[...] = (grad * u * s * (1.0 + a * (1.0 - s))).astype(bf16)
    du[...] = (grad * (a * s)).astype(bf16)

    for copy in p1_copies:
        copy.wait_recv()
    total = p1_in[0]
    for k in range(1, G):
        total = total + p1_in[k]
    p2_in[z] = total
    p2_copies = [
        send(p2_in.at[z], p2_in.at[z], p2_s.at[d], p2_r.at[d], in_z(d)) for d in range(1, NZ)
    ]

    loads[6].wait()
    loads[7].wait()

    @pl.loop(0, D // width)
    def _(j):
        here = pl.ds(pl.multiple_of(j * width, width), width)
        value = dot(dg[...], wg_v[here, :], NT) + dot(du[...], wu_v[here, :], NT)
        part[:, :, here] = value.astype(bf16).reshape(NY, rows, width)

    def give(k, src, to):
        sent.append(send(src, ig_in.at[k], ig_s.at[k], ig_r.at[k], to))
        return sent[-1]

    ig0 = give(0, part.at[y_opp, A], right)
    ig3 = give(3, part.at[y_opp, B], left)
    ig1 = give(1, part.at[y_right, B], right)
    ig4 = give(4, part.at[y_left, A], left)

    for copy in p2_copies:
        copy.wait_recv()
    total = p2_in[0]
    for k in range(1, NZ):
        total = total + p2_in[k]
    t_v[g] = total
    p3_copies = [
        send(t_v.at[g], t_v.at[g], p3_s.at[d], p3_r.at[d], in_group(d)) for d in range(1, G)
    ]

    @pl.loop(0, D // width)
    def _(j):
        here = pl.ds(pl.multiple_of(j * width, width), width)
        block = cbuf[:, :, here].reshape(TOK, width)
        m_v[:, here] = dot(hid_t[...], block) + e_v[:, here].astype(f32)

    for copy in p3_copies:
        copy.wait_recv()
    for copy in p3_copies:
        copy.wait_send()

    row_ids = lax.broadcasted_iota(jnp.int32, (RANK, 1), 0)
    tt[...] = t_v[...].reshape(RANK, F) * (1.0 / (NX * NZ * NC))

    def column(k, carry):
        vector = tt[pl.ds(k, 1), :]
        tile = tt[...]
        squares = jnp.sum(vector * vector, axis=1, keepdims=True) + epsilon
        factors = jnp.sum(tile * vector, axis=1, keepdims=True) * (1.0 / squares)
        tt[...] = tile - jnp.where(row_ids > k, factors, 0.0) * vector
        tt[pl.ds(k, 1), :] = vector * lax.rsqrt(squares)
        return carry

    lax.fori_loop(0, RANK, column, 0)
    left_copy = pltpu.make_async_copy(tt, left_out, out_s.at[0])
    left_copy.start()

    ts[...] = split(tt[...])
    zs[...] = split(fold(dot(ts[...], hid[...], NT)))

    r1_copies = []
    for h in range(HC):

        @pl.loop(0, D // HC // width)
        def _(j, h=h):
            start = pl.multiple_of(j * width, width)
            here = pl.ds(pl.multiple_of(h * (D // HC) + start, width), width)
            block = cbuf[:, :, here].reshape(TOK, width)
            value = fold(dot(zs[...], block) + dot(ts[...], e_v[:, here]))
            r1[pl.ds(4 * h, 4), :, pl.ds(start, width)] = value.astype(bf16).reshape(4, 16, width)

    for d in range(1, G):
        other = lax.rem(g + d, G)
        r1_copies.append(send(r1.at[other], r1_in.at[g], r1_s.at[d], r1_r.at[d], in_group(d)))
    r1_in[g] = r1[g]

    ig0.wait_recv()
    ig_sum[0] = (ig_in[0].astype(f32) + part[y_right, A].astype(f32)).astype(bf16)
    ig2 = give(2, ig_sum.at[0], right)
    ig3.wait_recv()
    ig_sum[1] = (ig_in[3].astype(f32) + part[y_left, B].astype(f32)).astype(bf16)
    ig5 = give(5, ig_sum.at[1], left)

    tt_both = jnp.concatenate([ts[:RANK].astype(f32), ts[RANK:].astype(f32)], axis=0).T.astype(bf16)

    for copy in r1_copies:
        copy.wait_recv()
    total = r1_in[0].astype(f32)
    for k in range(1, G):
        total = total + r1_in[k].astype(f32)
    for k in range(NZ):
        r2[k] = total[:, k * zw : (k + 1) * zw].astype(bf16)
    r2_copies = []
    for d in range(1, NZ):
        other = lax.rem(z + d, NZ)
        r2_copies.append(send(r2.at[other], r2_in.at[z], r2_s.at[d], r2_r.at[d], in_z(d)))
    r2_in[z] = r2[z]
    for copy in r2_copies:
        copy.wait_recv()
    total = r2_in[0].astype(f32)
    for k in range(1, NZ):
        total = total + r2_in[k].astype(f32)
    r3[z] = (total * (1.0 / (NX * NZ * NC))).astype(bf16)
    r3_copies = [
        send(r3.at[z], r3.at[z], r3_s.at[d], r3_r.at[d], in_z(d)) for d in range(1, NZ)
    ]
    for copy in r3_copies:
        copy.wait_recv()
    r4_copies = [
        send(r3, r4_in.at[g], r4_s.at[d], r4_r.at[d], in_group(d)) for d in range(1, G)
    ]
    r4_in[g] = r3[...]

    ig1.wait_recv()
    ig2.wait_recv()
    ig4.wait_recv()
    ig5.wait_recv()
    own_a = part[y, A].astype(f32) + ig_in[2].astype(f32) + ig_in[4].astype(f32)
    own_b = part[y, B].astype(f32) + ig_in[1].astype(f32) + ig_in[5].astype(f32)
    ig_v[A] = own_a.astype(bf16)
    ig_v[B] = own_b.astype(bf16)
    ig_copy = pltpu.make_async_copy(ig_v, ig, out_s.at[1])
    ig_copy.start()

    for copy in r4_copies:
        copy.wait_recv()

    for h in range(HC):

        @pl.loop(0, NZ)
        def _(k, h=h):
            here = pl.ds(pl.multiple_of(h * (D // HC) + k * zw, zw), zw)
            block = jnp.concatenate([r4_in[q + 4 * h, k] for q in range(4)], axis=0)
            right_v[:, here] = block.astype(f32)
            err_v[:, here] = (
                m_v[:, here] - dot(tt_both, jnp.concatenate([block, block], axis=0))
            ).astype(bf16)

    right_copy = pltpu.make_async_copy(right_v, right_out, out_s.at[2])
    right_copy.start()
    err_copy = pltpu.make_async_copy(err_v, err, out_s.at[3])
    err_copy.start()
    for copy in sent + p1_copies + p2_copies + r1_copies + r2_copies + r3_copies + r4_copies:
        copy.wait_send()
    for copy in (left_copy, ig_copy, right_copy, err_copy):
        copy.wait()


def shards(cotangent, gate_pre, up_pre, down_weight, gate_weight, up_weight, error_in, factor_in):
    G = NX * NC
    rows, D = cotangent.shape
    half = rows // 2
    TOK = NY * rows
    F = down_weight.shape[0]
    RANK = factor_in.shape[1]
    HC = G // 4
    zw = D // HC // NZ
    hw = D // HC
    VM = pltpu.VMEM
    DMA = pltpu.SemaphoreType.DMA
    scratch = [
        VM((NY, rows, D), bf16), VM((F, D), bf16), VM((D, F), bf16), VM((D, F), bf16),
        VM((F, D), bf16), VM((RANK, D), f32), VM((2 * RANK, D), bf16),
        VM((TOK, F), bf16), VM((TOK, F), bf16), VM((TOK, F), bf16), VM((F, TOK), bf16),
        VM((NY, rows, RANK), f32), VM((RANK, F), f32), VM((TOK, F), bf16), VM((TOK, F), bf16),
        VM((NY, rows, D), bf16), VM((6, half, D), bf16), VM((2, half, D), bf16), VM((rows, D), bf16),
        VM((G, RANK // G, F), f32), VM((G, RANK // G, F), f32), VM((NZ, RANK // G, F), f32),
        VM((G, RANK // G, F), f32), VM((2 * RANK, F), bf16), VM((RANK, F), f32),
        VM((2 * RANK, TOK), bf16), VM((F, D), f32),
        VM((G, 16, hw), bf16), VM((G, 16, hw), bf16), VM((NZ, 16, zw), bf16), VM((NZ, 16, zw), bf16),
        VM((NZ, 16, zw), bf16), VM((G, NZ, 16, zw), bf16), VM((RANK, D), f32), VM((F, D), bf16),
        DMA((8,)), DMA((6,)), DMA((6,)),
        DMA((G,)), DMA((G,)), DMA((NZ,)), DMA((NZ,)), DMA((G,)), DMA((G,)),
        DMA((G,)), DMA((G,)), DMA((NZ,)), DMA((NZ,)), DMA((NZ,)), DMA((NZ,)), DMA((G,)), DMA((G,)),
        DMA((6,)), DMA((6,)), DMA((4,)),
    ]
    shape = jax.ShapeDtypeStruct
    input_grad, left_t, right, error_out = pl.pallas_call(
        kernel,
        out_shape=(shape((rows, D), bf16), shape((RANK, F), f32), shape((RANK, D), f32), shape((F, D), bf16)),
        in_specs=[pl.BlockSpec(memory_space=pl.ANY)] * 8,
        out_specs=(pl.BlockSpec(memory_space=pl.ANY),) * 4,
        scratch_shapes=scratch,
        compiler_params=pltpu.CompilerParams(
            collective_id=0, has_side_effects=True, vmem_limit_bytes=48 * 1024 * 1024
        ),
        cost_estimate=pl.CostEstimate(flops=4 * 10**9, bytes_accessed=17 * 10**6, transcendentals=10**5),
    )(cotangent, gate_pre, up_pre, down_weight, gate_weight, up_weight, error_in[0], factor_in[0])
    return (input_grad, left_t.T, right[None], error_out[None])


def solution(mesh):
    in_specs = (
        P(("dp", "tensor"), None),
        P("dp", "tensor"),
        P("dp", "tensor"),
        P("tensor", None),
        P(None, "tensor"),
        P(None, "tensor"),
        P("dp", "tensor", None),
        P("tensor", None, None),
    )
    out_specs = (
        P(("dp", "tensor"), None),
        P("tensor", None),
        P("tensor", None, None),
        P("dp", "tensor", None),
    )
    return jax.shard_map(shards, mesh=mesh, in_specs=in_specs, out_specs=out_specs, check_vma=False)
```

time: 593 us -> 89.6 us (0.15)
  waiting for transfers between devices: 439 us -> 0 us
  Pallas kernels: 0 us -> 81 us
  other arithmetic: 50.7 us -> 0 us
  loops' own time: 46.7 us -> 0 us
  matrix products: 35.3 us -> 0 us
  between operations: 13.9 us -> 0.65 us
    psum x3 -> x0, waiting for transfers between devices: 399 us -> none  [the longest x1 177 us: shards(): right_sum = lax.psum(right_partial, 'dp') / replicas]
    pallas_call x0 -> x1, Pallas kernels: none -> 81 us  [shards(): pl.pallas_call(kernel, out_shape=(shape((rows, D), bf16), shape((RANK, F)...]
    another operation x1 -> x0, loops' own time: 46.7 us -> none  [orthonormal(): return lax.fori_loop(0, count_rows, step, matrix)]
    all_gather x1 -> x0, waiting for transfers between devices: 39.1 us -> none  [shards(): gathered = lax.all_gather(cotangent, 'tensor', axis=0, tiled=True)]
    reduce_sum x64 -> x0, other arithmetic: 38.9 us -> none  [step(): vector = vector / jnp.sqrt(jnp.sum(vector * vector) + epsilon)]
    dot_general x71 -> x0, matrix products: 35.3 us -> none  [the longest x64 8.89 us: step(): correlation = jnp.dot(current_tile, vector, precision=lax.Precision.HIGHEST)]
    sub x64 -> x0, other arithmetic: 7.17 us -> none  [step(): current_tile - jnp.where(later_rows, correlation, jnp.zeros_like(correlat...]
  transfers between devices with their start and end apart: 4 -> 0, of which waited for: 4 -> 0; matrix products, arithmetic and copies ran while one was open for 2% -> 0% of each run, Pallas kernels for 0% -> 0%
where the time goes in v1:
time: 89.6 us; the launch traced here: 89.4 us
  Pallas kernels  81 us (90%)
  local copies, waits for them, and re-layouts  7.78 us (9%)
    pallas_call x1, Pallas kernels, shards(): pl.pallas_call(kernel, out_shape=(shape((rows, D), bf16), shape((RANK, F)...  81 us
    unnamed x12, local copies, waits for them, and re-layouts  7.78 us

profile of v1, /device:TPU:1, one launch (start us, length us, event | category | flops | bytes accessed | tf_op | source)
XLA Modules:
  0.0 89.4 jit_solution(16938188549768991300)
XLA Ops:
  0.6 0.0 copy-start
  0.6 1.2 %copy-done = f32[1,64,4096]{2,1,0:T(8,128)S(1)} copy-done((f32[1,64,4096]{2,1,0:T(8,128)S(1)}, f32[1,64,4096]{2,1,0:T(8,128)}, u32[]{:S(2)}) %copy-start) | copy-done | bytes 1048600
  1.9 0.0 copy-start.1
  1.9 1.0 %copy-done.1 = bf16[64,4096]{1,0:T(8,128)(2,1)S(1)} copy-done((bf16[64,4096]{1,0:T(8,128)(2,1)S(1)}, bf16[64,4096]{1,0:T(8,128)(2,1)}, u32[]{:S(2)}) %copy-start.1) | copy-done | bytes 524312
  2.9 0.0 copy-start.2
  2.9 0.9 %copy-done.2 = bf16[256,256]{1,0:T(8,128)(2,1)S(1)} copy-done((bf16[256,256]{1,0:T(8,128)(2,1)S(1)}, bf16[256,256]{1,0:T(8,128)(2,1)}, u32[]{:S(2)}) %copy-start.2) | copy-done | bytes 131096
  3.8 0.0 copy-start.3
  3.8 0.9 %copy-done.3 = bf16[256,256]{1,0:T(8,128)(2,1)S(1)} copy-done((bf16[256,256]{1,0:T(8,128)(2,1)S(1)}, bf16[256,256]{1,0:T(8,128)(2,1)}, u32[]{:S(2)}) %copy-start.3) | copy-done | bytes 131096
  4.7 81.0 %shard_map.111 = (bf16[64,4096]{1,0:T(8,128)(2,1)S(1)}, f32[64,256]{1,0:T(8,128)S(1)}, f32[64,4096]{1,0:T(8,128)S(1)}, bf16[256,4096]{1,0:T(8,128)(2,1)S(1)}) custom-call(bf16[64,4096]{1,0:T(8,128)(2,1)S(1)} %copy-done.1, bf16[256,256]{1,0:T(8,128)(2,1)S(1)} %copy-done.2, bf16[256,256]{1,0:T(8,128)(2,1)S(1)} %copy-done.3, bf16[256,4096]{1,0:T(8,128)(2,1)} %wd.1, ...), custom_call_target="tpu_custom_call" | custom-call | flops 4000000000 | bytes 17000000 | tf_op jit(solution)/shard_map/pallas_call | solution.py:338
  85.7 0.8 copy.16
  86.5 0.6 copy.17
  87.1 1.0 %copy.18 = f32[1,64,4096]{2,1,0:T(8,128)} copy(f32[1,64,4096]{2,1,0:T(8,128)S(1)} %bitcast.6) | data formatting | bytes 2097152
  88.1 1.3 %copy.19 = bf16[1,256,4096]{2,1,0:T(8,128)(2,1)} copy(bf16[1,256,4096]{2,1,0:T(8,128)(2,1)S(1)} %bitcast.5) | data formatting | bytes 4194304
Async XLA Ops:
  0.6 1.2 %copy-start = (f32[1,64,4096]{2,1,0:T(8,128)S(1)}, f32[1,64,4096]{2,1,0:T(8,128)}, u32[]{:S(2)}) copy-start(f32[1,64,4096]{2,1,0:T(8,128)} %param.15) | copy-start | bytes 3145732
  1.9 1.0 %copy-start.1 = (bf16[64,4096]{1,0:T(8,128)(2,1)S(1)}, bf16[64,4096]{1,0:T(8,128)(2,1)}, u32[]{:S(2)}) copy-start(bf16[64,4096]{1,0:T(8,128)(2,1)} %c.1) | copy-start | bytes 1572868
  2.9 0.9 %copy-start.2 = (bf16[256,256]{1,0:T(8,128)(2,1)S(1)}, bf16[256,256]{1,0:T(8,128)(2,1)}, u32[]{:S(2)}) copy-start(bf16[256,256]{1,0:T(8,128)(2,1)} %gate.1) | copy-start | bytes 393220
  3.8 0.9 %copy-start.3 = (bf16[256,256]{1,0:T(8,128)(2,1)S(1)}, bf16[256,256]{1,0:T(8,128)(2,1)}, u32[]{:S(2)}) copy-start(bf16[256,256]{1,0:T(8,128)(2,1)} %up.1) | copy-start | bytes 393220

commit v2 on v1

v2 whole, which is shorter than its diff:
```python
import functools

import jax
import jax.numpy as jnp
from jax import lax
from jax.experimental import pallas as pl
from jax.experimental.pallas import tpu as pltpu
from jax.sharding import PartitionSpec as P

epsilon = 1e-06
NX, NZ, NC = 4, 8, 2
NY = 4
VMEM_MIB = 57
MESH = pl.DeviceIdType.MESH
f32, bf16 = jnp.float32, jnp.bfloat16
NN = (((1,), (0,)), ((), ()))
NT = (((1,), (1,)), ((), ()))


def dot(a, b, dims=NN):
    return lax.dot_general(a, b, dims, preferred_element_type=f32)


def split(a):
    high = a.astype(bf16)
    low = (a - high.astype(f32)).astype(bf16)
    return jnp.concatenate([high, low], axis=0)


def fold(a):
    half = a.shape[0] // 2
    return a[:half] + a[half:]


def kernel(
    c, gate, up, wd, wg, wu, e, f,
    ig_v, tt, rfull, m_v,
    cbuf, wd_v, wg_v, wu_v, e_v, f_v, fs, gate_v, up_v, hid, hid_t, y_v, pe, dg, du,
    part, ig_in, ig_sum,
    p1, p1_in, p2_in, t_v, ts, mc, mc_in, mx, mx_in, r2, r2_in,
    load, ag_s, ag_r, p1_s, p1_r, p2_s, p2_r, p3_s, p3_r,
    mc_s, mc_r, mx_s, mx_r, r2_s, r2_r, r3_s, r3_r, r4_s, r4_r, r5_s, r5_r, ig_s, ig_r,
):
    G = NX * NC
    rows, D = c.shape
    half = rows // 2
    TOK = NY * rows
    F = wd.shape[0]
    RANK = f.shape[0]
    hw = D // NC
    xw = hw // NX
    zw = xw // (NZ // 4)
    width = min(1024, hw)
    mean = 1.0 / (NX * NZ * NC)

    dp, y = lax.axis_index("dp"), lax.axis_index("tensor")
    core = lax.rem(dp, NC)
    z = lax.rem(dp // NC, NZ)
    x = dp // (NC * NZ)
    g = x * NC + core
    y_right, y_left, y_opp = (lax.rem(y + k, NY) for k in (1, 3, 2))

    def in_group(d):
        other = lax.rem(g + d, G)
        return (((other // NC) * NZ + z) * NC + lax.rem(other, NC), y)

    def in_x(d):
        return ((lax.rem(x + d, NX) * NZ + z) * NC + core, y)

    def in_z(d):
        return ((x * NZ + lax.rem(z + d, NZ)) * NC + core, y)

    sibling = (dp + 1 - 2 * core, y)

    mine = cbuf.at[y]
    pairs = [(c, mine), (f, f_v), (e, e_v), (gate, gate_v), (up, up_v), (wd, wd_v), (wg, wg_v), (wu, wu_v)]
    loads = [pltpu.make_async_copy(a, b, load.at[k]) for k, (a, b) in enumerate(pairs)]
    for copy in loads:
        copy.start()

    barrier = pltpu.get_barrier_semaphore()
    partners = [(dp, y_right), (dp, y_left)]
    partners += [in_group(d) for d in range(1, G)] + [in_z(d) for d in range(1, NZ)]
    for other in partners:
        pl.semaphore_signal(barrier, inc=1, device_id=other, device_id_type=MESH)
    pl.semaphore_wait(barrier, len(partners))

    sent = []

    def send(src, dst, s, r, to):
        copy = pltpu.make_async_remote_copy(
            src_ref=src, dst_ref=dst, send_sem=s, recv_sem=r, device_id=to, device_id_type=MESH
        )
        copy.start()
        sent.append(copy)
        return copy

    right, left = (dp, y_right), (dp, y_left)
    A, B = pl.ds(0, half), pl.ds(half, half)

    def gather(k, src, dst, to):
        return send(src, dst, ag_s.at[k], ag_r.at[k], to)

    from_left_a = gather(0, c.at[A], cbuf.at[y, A], right)
    from_right_b = gather(1, c.at[B], cbuf.at[y, B], left)

    loads[1].wait()
    fs[...] = split(f_v[...])
    loads[0].wait()

    def tokens_times_factor(slot):
        both = dot(cbuf[slot], fs[...], NT)
        y_v[slot] = both[:, :RANK] + both[:, RANK:]

    tokens_times_factor(y)
    loads[2].wait()
    pe[...] = fold(dot(fs[...], e_v[...], NT))

    from_left_b = gather(2, c.at[B], cbuf.at[y, B], right)
    from_right_a = gather(3, c.at[A], cbuf.at[y, A], left)

    loads[3].wait()
    loads[4].wait()
    a, u = gate_v[...].astype(f32), up_v[...].astype(f32)
    hidden = a * jax.nn.sigmoid(a) * u
    hidden = hidden.astype(bf16).astype(f32)
    hid[...] = hidden.astype(bf16)
    hid_t[...] = hidden.T.astype(bf16)

    from_left_a.wait_recv()
    from_opp_a = gather(4, cbuf.at[y_left, A], cbuf.at[y_left, A], right)
    from_right_b.wait_recv()
    from_opp_b = gather(5, cbuf.at[y_right, B], cbuf.at[y_right, B], left)
    from_left_b.wait_recv()
    tokens_times_factor(y_left)
    from_right_a.wait_recv()
    tokens_times_factor(y_right)
    for k in (5, 6, 7):
        loads[k].wait()
    from_opp_a.wait_recv()
    from_opp_b.wait_recv()
    tokens_times_factor(y_opp)

    y_all = y_v[...].reshape(TOK, RANK)
    y_high = y_all.astype(bf16).astype(f32)
    y_both = jnp.concatenate([y_high, y_all - y_high], axis=1).T.astype(bf16)
    p_all = fold(dot(y_both, hid[...])) + pe[...]
    p1[...] = p_all.reshape(NZ, RANK // NZ, F)
    p1_copies = []
    for d in range(1, NZ):
        other = lax.rem(z + d, NZ)
        p1_copies.append(send(p1.at[other], p1_in.at[z], p1_s.at[d], p1_r.at[d], in_z(d)))
    p1_in[z] = p1[z]

    def weight_gradient(first, j):
        here = pl.ds(pl.multiple_of(first + j * width, width), width)
        block = cbuf[:, :, here].reshape(TOK, width)
        value = dot(hid_t[...], block) + e_v[:, here].astype(f32)
        m_v[:, here] = value
        return value

    for j in range(hw // width):
        mc[:, j * width : (j + 1) * width] = weight_gradient((1 - core) * hw, j).astype(bf16)
    mc_copy = send(mc, mc_in, mc_s.at[0], mc_r.at[0], sibling)
    for j in range(hw // width):
        weight_gradient(core * hw, j)

    grad = dot(cbuf[...].reshape(TOK, D), wd_v[...], NT)
    a, u = gate_v[...].astype(f32), up_v[...].astype(f32)
    s = jax.nn.sigmoid(a)
    dg[...] = (grad * u * s * (1.0 + a * (1.0 - s))).astype(bf16)
    du[...] = (grad * (a * s)).astype(bf16)
    for j in range(D // width):
        here = pl.ds(j * width, width)
        value = dot(dg[...], wg_v[here, :], NT) + dot(du[...], wu_v[here, :], NT)
        part[:, :, here] = value.astype(bf16).reshape(NY, rows, width)

    def give(k, src, to):
        return send(src, ig_in.at[k], ig_s.at[k], ig_r.at[k], to)

    ig0 = give(0, part.at[y_opp, A], right)
    ig3 = give(3, part.at[y_opp, B], left)

    def total_of(ref, count):
        total = ref[0].astype(f32)
        for k in range(1, count):
            total = total + ref[k].astype(f32)
        return total

    for copy in p1_copies:
        copy.wait_recv()
    p2_in[g] = total_of(p1_in, NZ)
    p2_copies = [
        send(p2_in.at[g], p2_in.at[g], p2_s.at[d], p2_r.at[d], in_group(d)) for d in range(1, G)
    ]
    ig1 = give(1, part.at[y_right, B], right)
    ig4 = give(4, part.at[y_left, A], left)

    mc_copy.wait_recv()
    for k in range(NX):
        here = pl.ds(pl.multiple_of(core * hw + k * xw, xw), xw)
        mx[k] = (m_v[:, here] + mc_in[:, k * xw : (k + 1) * xw].astype(f32)).astype(bf16)
    mx_copies = []
    for d in range(1, NX):
        other = lax.rem(x + d, NX)
        mx_copies.append(send(mx.at[other], mx_in.at[x], mx_s.at[d], mx_r.at[d], in_x(d)))
    mx_in[x] = mx[x]

    for copy in p2_copies:
        copy.wait_recv()
    for copy in p2_copies:
        copy.wait_send()
    t_v[z] = total_of(p2_in, G)
    p3_copies = [
        send(t_v.at[z], t_v.at[z], p3_s.at[d], p3_r.at[d], in_z(d)) for d in range(1, NZ)
    ]
    for copy in p3_copies:
        copy.wait_recv()

    row_ids = lax.broadcasted_iota(jnp.int32, (RANK, 1), 0)
    tt[...] = t_v[...].reshape(RANK, F) * mean

    def column(k, carry):
        vector = tt[pl.ds(k, 1), :]
        tile = tt[...]
        squares = jnp.sum(vector * vector, axis=1, keepdims=True) + epsilon
        factors = jnp.sum(tile * vector, axis=1, keepdims=True) * (1.0 / squares)
        tt[...] = tile - jnp.where(row_ids > k, factors, 0.0) * vector
        tt[pl.ds(k, 1), :] = vector * lax.rsqrt(squares)
        return carry

    lax.fori_loop(0, RANK, column, 0)
    ts[...] = split(tt[...])

    for copy in mx_copies:
        copy.wait_recv()
    m_sum = total_of(mx_in, NX)
    m_high = m_sum.astype(bf16)
    m_low = (m_sum - m_high.astype(f32)).astype(bf16)
    r_all = fold(dot(ts[...], m_high)) + dot(ts[:RANK], m_low)
    for k in range(NZ):
        q, h = k % 4, k // 4
        r2[k] = r_all[16 * q : 16 * q + 16, h * zw : (h + 1) * zw].astype(bf16)
    r2_copies = []
    for d in range(1, NZ):
        other = lax.rem(z + d, NZ)
        r2_copies.append(send(r2.at[other], r2_in.at[z], r2_s.at[d], r2_r.at[d], in_z(d)))
    r2_in[z] = r2[z]

    ig0.wait_recv()
    ig_sum[0] = (ig_in[0].astype(f32) + part[y_right, A].astype(f32)).astype(bf16)
    ig2 = give(2, ig_sum.at[0], right)
    ig3.wait_recv()
    ig_sum[1] = (ig_in[3].astype(f32) + part[y_left, B].astype(f32)).astype(bf16)
    ig5 = give(5, ig_sum.at[1], left)

    for copy in r2_copies:
        copy.wait_recv()
    rfull[core, x, z] = (total_of(r2_in, NZ) * mean).astype(bf16)
    own = rfull.at[core, x, z]
    r3_copies = [send(own, own, r3_s.at[d], r3_r.at[d], in_z(d)) for d in range(1, NZ)]
    for copy in r3_copies:
        copy.wait_recv()
    own = rfull.at[core, x]
    r4_copies = [send(own, own, r4_s.at[d], r4_r.at[d], in_x(d)) for d in range(1, NX)]
    r5_copies = [send(own, own, r5_s.at[0], r5_r.at[0], sibling)]

    ig1.wait_recv()
    ig4.wait_recv()
    ig2.wait_recv()
    own_a = part[y, A].astype(f32) + ig_in[2].astype(f32) + ig_in[4].astype(f32)
    ig_v[A] = own_a.astype(bf16)
    ig5.wait_recv()
    own_b = part[y, B].astype(f32) + ig_in[1].astype(f32) + ig_in[5].astype(f32)
    ig_v[B] = own_b.astype(bf16)

    for d in range(1, NX):
        r4_copies[d - 1].wait_recv()
        came = rfull.at[core, lax.rem(x + NX - d, NX)]
        r5_copies.append(send(came, came, r5_s.at[d], r5_r.at[d], sibling))
    for copy in r5_copies:
        copy.wait_recv()
    for copy in sent:
        if not any(copy is done for done in p2_copies):
            copy.wait_send()


def finish(ig_v, tt, rfull, m_v, ig, left_out, right_out, err, right_v, err_v, sems):
    RANK, F = tt.shape
    D = m_v.shape[1]
    hw = D // NC
    xw = hw // NX
    zw = xw // (NZ // 4)
    copies = [
        pltpu.make_async_copy(ig_v, ig, sems.at[0]),
        pltpu.make_async_copy(tt, left_out, sems.at[1]),
    ]
    for copy in copies:
        copy.start()
    high = tt[...].astype(bf16).astype(f32)
    both = jnp.concatenate([high, tt[...] - high], axis=0).T.astype(bf16)
    for k in range(NC * NX):
        first = k * xw
        blocks = []
        for h in range(NZ // 4):
            rows = [rfull[k // NX, k % NX, 4 * h + q] for q in range(4)]
            blocks.append(jnp.concatenate(rows, axis=0))
        block = jnp.concatenate(blocks, axis=1)
        here = pl.ds(first, xw)
        right_v[:, here] = block.astype(f32)
        update = dot(both, jnp.concatenate([block, block], axis=0))
        err_v[:, here] = (m_v[:, here] - update).astype(bf16)
        copies.append(pltpu.make_async_copy(err_v.at[:, here], err.at[:, here], sems.at[3 + k]))
        copies[-1].start()
    copies.append(pltpu.make_async_copy(right_v, right_out, sems.at[2]))
    copies[-1].start()
    for copy in copies:
        copy.wait()


def shards(cotangent, gate_pre, up_pre, down_weight, gate_weight, up_weight, error_in, factor_in):
    G = NX * NC
    rows, D = cotangent.shape
    half = rows // 2
    TOK = NY * rows
    F = down_weight.shape[0]
    RANK = factor_in.shape[1]
    hw = D // NC
    xw = hw // NX
    zw = xw // (NZ // 4)
    VM = pltpu.VMEM
    DMA = pltpu.SemaphoreType.DMA
    piece = RANK // NZ
    scratch = [
        VM((NY, rows, D), bf16), VM((F, D), bf16), VM((D, F), bf16), VM((D, F), bf16),
        VM((F, D), bf16), VM((RANK, D), f32), VM((2 * RANK, D), bf16),
        VM((TOK, F), bf16), VM((TOK, F), bf16), VM((TOK, F), bf16), VM((F, TOK), bf16),
        VM((NY, rows, RANK), f32), VM((RANK, F), f32), VM((TOK, F), bf16), VM((TOK, F), bf16),
        VM((NY, rows, D), bf16), VM((6, half, D), bf16), VM((2, half, D), bf16),
        VM((NZ, piece, F), f32), VM((NZ, piece, F), f32), VM((G, piece, F), f32), VM((NZ, piece, F), f32),
        VM((2 * RANK, F), bf16), VM((F, hw), bf16), VM((F, hw), bf16),
        VM((NX, F, xw), bf16), VM((NX, F, xw), bf16), VM((NZ, 16, zw), bf16), VM((NZ, 16, zw), bf16),
        DMA((8,)), DMA((6,)), DMA((6,)),
        DMA((NZ,)), DMA((NZ,)), DMA((G,)), DMA((G,)), DMA((NZ,)), DMA((NZ,)),
        DMA((1,)), DMA((1,)), DMA((NX,)), DMA((NX,)), DMA((NZ,)), DMA((NZ,)), DMA((NZ,)), DMA((NZ,)),
        DMA((NX,)), DMA((NX,)), DMA((NX,)), DMA((NX,)), DMA((6,)), DMA((6,)),
    ]
    in_vmem = pl.BlockSpec(memory_space=pltpu.VMEM)
    anywhere = pl.BlockSpec(memory_space=pl.ANY)
    held = pl.pallas_call(
        kernel,
        out_shape=(VM((rows, D), bf16), VM((RANK, F), f32), VM((NC, NX, NZ, 16, zw), bf16), VM((F, D), f32)),
        in_specs=[anywhere] * 8,
        out_specs=(in_vmem,) * 4,
        scratch_shapes=scratch,
        compiler_params=pltpu.CompilerParams(
            collective_id=0, has_side_effects=True, vmem_limit_bytes=VMEM_MIB * 1024 * 1024
        ),
        cost_estimate=pl.CostEstimate(flops=4 * 10**9, bytes_accessed=17 * 10**6, transcendentals=10**5),
    )(cotangent, gate_pre, up_pre, down_weight, gate_weight, up_weight, error_in[0], factor_in[0])
    shape = jax.ShapeDtypeStruct
    input_grad, left_t, right, error_out = pl.pallas_call(
        finish,
        out_shape=(shape((rows, D), bf16), shape((RANK, F), f32), shape((RANK, D), f32), shape((F, D), bf16)),
        in_specs=[in_vmem] * 4,
        out_specs=(anywhere,) * 4,
        scratch_shapes=[VM((RANK, D), f32), VM((F, D), bf16), DMA((3 + NC * NX,))],
        compiler_params=pltpu.CompilerParams(vmem_limit_bytes=16 * 1024 * 1024),
        cost_estimate=pl.CostEstimate(flops=3 * 10**8, bytes_accessed=9 * 10**6, transcendentals=0),
    )(*held)
    return (input_grad, left_t.T, right[None], error_out[None])


def solution(mesh):
    in_specs = (
        P(("dp", "tensor"), None),
        P("dp", "tensor"),
        P("dp", "tensor"),
        P("tensor", None),
        P(None, "tensor"),
        P(None, "tensor"),
        P("dp", "tensor", None),
        P("tensor", None, None),
    )
    out_specs = (
        P(("dp", "tensor"), None),
        P("tensor", None),
        P("tensor", None, None),
        P("dp", "tensor", None),
    )
    return jax.shard_map(shards, mesh=mesh, in_specs=in_specs, out_specs=out_specs, check_vma=False)
```

time: 89.6 us -> 72 us (0.80)
  Pallas kernels: 81 us -> 71.3 us
  local copies, waits for them, and re-layouts: 7.78 us -> 0 us
    pallas_call x1 -> x2, Pallas kernels: 81 us -> 71.3 us  [the longest x1 69.2 us: shards(): pl.pallas_call(kernel, out_shape=(VM((rows, D), bf16), VM((RANK, F), f32)...]
    unnamed x12 -> x0, local copies, waits for them, and re-layouts: 7.78 us -> none
where the time goes in v2:
time: 72 us; the launch traced here: 71.9 us
  Pallas kernels  71.3 us (99%)
    pallas_call x1, Pallas kernels, shards(): pl.pallas_call(kernel, out_shape=(VM((rows, D), bf16), VM((RANK, F), f32)...  69.2 us
    pallas_call x1, Pallas kernels, shards(): pl.pallas_call(finish, out_shape=(shape((rows, D), bf16), shape((RANK, F)...  2.03 us

profile of v2, /device:TPU:1, one launch (start us, length us, event | category | flops | bytes accessed | tf_op | source)
XLA Modules:
  0.0 71.9 jit_solution(1929181618941870714)
XLA Ops:
  0.6 69.2 %shard_map.111 = (bf16[64,4096]{1,0:T(8,128)(2,1)S(1)}, f32[64,256]{1,0:T(8,128)S(1)}, bf16[2,4,8,16,256]{4,3,2,1,0:T(8,128)(2,1)S(1)}, f32[256,4096]{1,0:T(8,128)S(1)}) custom-call(bf16[64,4096]{1,0:T(8,128)(2,1)} %c.1, bf16[256,256]{1,0:T(8,128)(2,1)} %gate.1, bf16[256,256]{1,0:T(8,128)(2,1)} %up.1, bf16[256,4096]{1,0:T(8,128)(2,1)} %wd.1, ...), custom_call_target="tpu_custom_call" | custom-call | flops 4000000000 | bytes 17000000 | tf_op jit(solution)/shard_map/pallas_call | solution.py:350
  69.9 2.0 %shard_map.112 = (bf16[64,4096]{1,0:T(8,128)(2,1)}, f32[64,256]{1,0:T(8,128)}, f32[64,4096]{1,0:T(8,128)}, bf16[256,4096]{1,0:T(8,128)(2,1)}) custom-call(bf16[64,4096]{1,0:T(8,128)(2,1)S(1)} %get-tuple-element.12.ig_v, f32[64,256]{1,0:T(8,128)S(1)} %get-tuple-element.13.tt, bf16[2,4,8,16,256]{4,3,2,1,0:T(8,128)(2,1)S(1)} %get-tuple-element.14.rfull, ...), custom_call_target="tpu_custom_call" | custom-call | flops 300000000 | bytes 9000000 | tf_op jit(solution)/shard_map/pallas_call | solution.py:362

commit v3 on v2

--- a/solution.py
+++ b/solution.py
@@ -72,6 +72,10 @@
 
     sibling = (dp + 1 - 2 * core, y)
 
+    z_far = sorted(range(1, NZ), key=lambda d: -min(d, NZ - d))
+    x_far = sorted(range(1, NX), key=lambda d: -min(d, NX - d))
+    g_far = sorted(range(1, G), key=lambda d: -min(d // NC, NX - d // NC))
+
     mine = cbuf.at[y]
     pairs = [(c, mine), (f, f_v), (e, e_v), (gate, gate_v), (up, up_v), (wd, wd_v), (wg, wg_v), (wu, wu_v)]
     loads = [pltpu.make_async_copy(a, b, load.at[k]) for k, (a, b) in enumerate(pairs)]
@@ -147,7 +151,7 @@
     p_all = fold(dot(y_both, hid[...])) + pe[...]
     p1[...] = p_all.reshape(NZ, RANK // NZ, F)
     p1_copies = []
-    for d in range(1, NZ):
+    for d in z_far:
         other = lax.rem(z + d, NZ)
         p1_copies.append(send(p1.at[other], p1_in.at[z], p1_s.at[d], p1_r.at[d], in_z(d)))
     p1_in[z] = p1[z]
@@ -170,50 +174,45 @@
     s = jax.nn.sigmoid(a)
     dg[...] = (grad * u * s * (1.0 + a * (1.0 - s))).astype(bf16)
     du[...] = (grad * (a * s)).astype(bf16)
-    for j in range(D // width):
-        here = pl.ds(j * width, width)
-        value = dot(dg[...], wg_v[here, :], NT) + dot(du[...], wu_v[here, :], NT)
-        part[:, :, here] = value.astype(bf16).reshape(NY, rows, width)
-
-    def give(k, src, to):
-        return send(src, ig_in.at[k], ig_s.at[k], ig_r.at[k], to)
-
-    ig0 = give(0, part.at[y_opp, A], right)
-    ig3 = give(3, part.at[y_opp, B], left)
-
     def total_of(ref, count):
         total = ref[0].astype(f32)
         for k in range(1, count):
             total = total + ref[k].astype(f32)
         return total
 
-    for copy in p1_copies:
-        copy.wait_recv()
-    p2_in[g] = total_of(p1_in, NZ)
-    p2_copies = [
-        send(p2_in.at[g], p2_in.at[g], p2_s.at[d], p2_r.at[d], in_group(d)) for d in range(1, G)
-    ]
-    ig1 = give(1, part.at[y_right, B], right)
-    ig4 = give(4, part.at[y_left, A], left)
-
     mc_copy.wait_recv()
     for k in range(NX):
         here = pl.ds(pl.multiple_of(core * hw + k * xw, xw), xw)
         mx[k] = (m_v[:, here] + mc_in[:, k * xw : (k + 1) * xw].astype(f32)).astype(bf16)
+
+    for copy in p1_copies:
+        copy.wait_recv()
+    p2_in[g] = total_of(p1_in, NZ)
+    p2_copies = [send(p2_in.at[g], p2_in.at[g], p2_s.at[d], p2_r.at[d], in_group(d)) for d in g_far]
+
     mx_copies = []
-    for d in range(1, NX):
+    for d in x_far:
         other = lax.rem(x + d, NX)
         mx_copies.append(send(mx.at[other], mx_in.at[x], mx_s.at[d], mx_r.at[d], in_x(d)))
+
+    for j in range(D // width):
+        here = pl.ds(j * width, width)
+        value = dot(dg[...], wg_v[here, :], NT) + dot(du[...], wu_v[here, :], NT)
+        part[:, :, here] = value.astype(bf16).reshape(NY, rows, width)
+
+    def give(k, src, to):
+        return send(src, ig_in.at[k], ig_s.at[k], ig_r.at[k], to)
+
+    ig0 = give(0, part.at[y_opp, A], right)
+    ig3 = give(3, part.at[y_opp, B], left)
+    ig1 = give(1, part.at[y_right, B], right)
+    ig4 = give(4, part.at[y_left, A], left)
     mx_in[x] = mx[x]
 
     for copy in p2_copies:
         copy.wait_recv()
-    for copy in p2_copies:
-        copy.wait_send()
     t_v[z] = total_of(p2_in, G)
-    p3_copies = [
-        send(t_v.at[z], t_v.at[z], p3_s.at[d], p3_r.at[d], in_z(d)) for d in range(1, NZ)
-    ]
+    p3_copies = [send(t_v.at[z], t_v.at[z], p3_s.at[d], p3_r.at[d], in_z(d)) for d in z_far]
     for copy in p3_copies:
         copy.wait_recv()
 
@@ -242,7 +241,7 @@
         q, h = k % 4, k // 4
         r2[k] = r_all[16 * q : 16 * q + 16, h * zw : (h + 1) * zw].astype(bf16)
     r2_copies = []
-    for d in range(1, NZ):
+    for d in z_far:
         other = lax.rem(z + d, NZ)
         r2_copies.append(send(r2.at[other], r2_in.at[z], r2_s.at[d], r2_r.at[d], in_z(d)))
     r2_in[z] = r2[z]
@@ -254,15 +253,30 @@
     ig_sum[1] = (ig_in[3].astype(f32) + part[y_left, B].astype(f32)).astype(bf16)
     ig5 = give(5, ig_sum.at[1], left)
 
+    def all_left():
+        for copy in sent:
+            copy.wait_send()
+        sent.clear()
+
+    all_left()
     for copy in r2_copies:
         copy.wait_recv()
     rfull[core, x, z] = (total_of(r2_in, NZ) * mean).astype(bf16)
     own = rfull.at[core, x, z]
-    r3_copies = [send(own, own, r3_s.at[d], r3_r.at[d], in_z(d)) for d in range(1, NZ)]
-    for copy in r3_copies:
-        copy.wait_recv()
+    r3_copies = {d: send(own, own, r3_s.at[d], r3_r.at[d], in_z(d)) for d in z_far}
+
+    r4_copies = {}
+
+    def along_x(k):
+        piece = rfull.at[core, x, lax.rem(z + NZ - k, NZ)]
+        for d in x_far:
+            r4_copies[d, k] = send(piece, piece, r4_s.at[d, k], r4_r.at[d, k], in_x(d))
+
+    along_x(0)
+    for k in reversed(z_far):
+        r3_copies[k].wait_recv()
+        along_x(k)
     own = rfull.at[core, x]
-    r4_copies = [send(own, own, r4_s.at[d], r4_r.at[d], in_x(d)) for d in range(1, NX)]
     r5_copies = [send(own, own, r5_s.at[0], r5_r.at[0], sibling)]
 
     ig1.wait_recv()
@@ -274,15 +288,14 @@
     own_b = part[y, B].astype(f32) + ig_in[1].astype(f32) + ig_in[5].astype(f32)
     ig_v[B] = own_b.astype(bf16)
 
-    for d in range(1, NX):
-        r4_copies[d - 1].wait_recv()
+    for d in reversed(x_far):
+        for k in range(NZ):
+            r4_copies[d, k].wait_recv()
         came = rfull.at[core, lax.rem(x + NX - d, NX)]
         r5_copies.append(send(came, came, r5_s.at[d], r5_r.at[d], sibling))
     for copy in r5_copies:
         copy.wait_recv()
-    for copy in sent:
-        if not any(copy is done for done in p2_copies):
-            copy.wait_send()
+    all_left()
 
 
 def finish(ig_v, tt, rfull, m_v, ig, left_out, right_out, err, right_v, err_v, sems):
@@ -343,7 +356,7 @@
         DMA((8,)), DMA((6,)), DMA((6,)),
         DMA((NZ,)), DMA((NZ,)), DMA((G,)), DMA((G,)), DMA((NZ,)), DMA((NZ,)),
         DMA((1,)), DMA((1,)), DMA((NX,)), DMA((NX,)), DMA((NZ,)), DMA((NZ,)), DMA((NZ,)), DMA((NZ,)),
-        DMA((NX,)), DMA((NX,)), DMA((NX,)), DMA((NX,)), DMA((6,)), DMA((6,)),
+        DMA((NX, NZ)), DMA((NX, NZ)), DMA((NX,)), DMA((NX,)), DMA((6,)), DMA((6,)),
     ]
     in_vmem = pl.BlockSpec(memory_space=pltpu.VMEM)
     anywhere = pl.BlockSpec(memory_space=pl.ANY)

time: 72 us -> 73.1 us (1.015)
  Pallas kernels: 71.3 us -> 72.4 us
    pallas_call x1, Pallas kernels: 69.2 us -> 70.4 us  [shards(): pl.pallas_call(kernel, out_shape=(VM((rows, D), bf16), VM((RANK, F), f32)...]
where the time goes in v3:
time: 73.1 us
  Pallas kernels  72.4 us (99%)
    pallas_call x1, Pallas kernels, shards(): pl.pallas_call(kernel, out_shape=(VM((rows, D), bf16), VM((RANK, F), f32)...  70.4 us
    pallas_call x1, Pallas kernels, shards(): pl.pallas_call(finish, out_shape=(shape((rows, D), bf16), shape((RANK, F)...  2.03 us

profile of v3, /device:TPU:1, one launch (start us, length us, event | category | flops | bytes accessed | tf_op | source)
XLA Modules:
  0.0 73.1 jit_solution(18230213169938744434)
XLA Ops:
  0.6 70.4 %shard_map.111 = (bf16[64,4096]{1,0:T(8,128)(2,1)S(1)}, f32[64,256]{1,0:T(8,128)S(1)}, bf16[2,4,8,16,256]{4,3,2,1,0:T(8,128)(2,1)S(1)}, f32[256,4096]{1,0:T(8,128)S(1)}) custom-call(bf16[64,4096]{1,0:T(8,128)(2,1)} %c.1, bf16[256,256]{1,0:T(8,128)(2,1)} %gate.1, bf16[256,256]{1,0:T(8,128)(2,1)} %up.1, bf16[256,4096]{1,0:T(8,128)(2,1)} %wd.1, ...), custom_call_target="tpu_custom_call" | custom-call | flops 4000000000 | bytes 17000000 | tf_op jit(solution)/shard_map/pallas_call | solution.py:363
  71.0 2.0 %shard_map.112 = (bf16[64,4096]{1,0:T(8,128)(2,1)}, f32[64,256]{1,0:T(8,128)}, f32[64,4096]{1,0:T(8,128)}, bf16[256,4096]{1,0:T(8,128)(2,1)}) custom-call(bf16[64,4096]{1,0:T(8,128)(2,1)S(1)} %get-tuple-element.12.ig_v, f32[64,256]{1,0:T(8,128)S(1)} %get-tuple-element.13.tt, bf16[2,4,8,16,256]{4,3,2,1,0:T(8,128)(2,1)S(1)} %get-tuple-element.14.rfull, ...), custom_call_target="tpu_custom_call" | custom-call | flops 300000000 | bytes 9000000 | tf_op jit(solution)/shard_map/pallas_call | solution.py:375

commit v4 on v3

--- a/solution.py
+++ b/solution.py
@@ -11,6 +11,7 @@
 NX, NZ, NC = 4, 8, 2
 NY = 4
 VMEM_MIB = 57
+NQ = 4
 MESH = pl.DeviceIdType.MESH
 f32, bf16 = jnp.float32, jnp.bfloat16
 NN = (((1,), (0,)), ((), ()))
@@ -48,8 +49,9 @@
     F = wd.shape[0]
     RANK = f.shape[0]
     hw = D // NC
-    xw = hw // NX
-    zw = xw // (NZ // 4)
+    qw = hw // NQ
+    pw = qw // NX
+    zw = NQ * pw // (NZ // 4)
     width = min(1024, hw)
     mean = 1.0 / (NX * NZ * NC)
 
@@ -156,63 +158,80 @@
         p1_copies.append(send(p1.at[other], p1_in.at[z], p1_s.at[d], p1_r.at[d], in_z(d)))
     p1_in[z] = p1[z]
 
-    def weight_gradient(first, j):
-        here = pl.ds(pl.multiple_of(first + j * width, width), width)
-        block = cbuf[:, :, here].reshape(TOK, width)
+    def weight_gradient(first):
+        here = pl.ds(pl.multiple_of(first, qw), qw)
+        block = cbuf[:, :, here].reshape(TOK, qw)
         value = dot(hid_t[...], block) + e_v[:, here].astype(f32)
         m_v[:, here] = value
         return value
 
-    for j in range(hw // width):
-        mc[:, j * width : (j + 1) * width] = weight_gradient((1 - core) * hw, j).astype(bf16)
-    mc_copy = send(mc, mc_in, mc_s.at[0], mc_r.at[0], sibling)
-    for j in range(hw // width):
-        weight_gradient(core * hw, j)
+    rest = pl.ds(1, NQ - 1)
+    mc[0] = weight_gradient((1 - core) * hw).astype(bf16)
+    mc_first = send(mc.at[0], mc_in.at[0], mc_s.at[0], mc_r.at[0], sibling)
+    for q in range(1, NQ):
+        mc[q] = weight_gradient((1 - core) * hw + q * qw).astype(bf16)
+    mc_rest = send(mc.at[rest], mc_in.at[rest], mc_s.at[1], mc_r.at[1], sibling)
+    for q in range(NQ):
+        weight_gradient(core * hw + q * qw)
+
+    def chip_sum(q):
+        for k in range(NX):
+            here = pl.ds(pl.multiple_of(core * hw + q * qw + k * pw, pw), pw)
+            mx[k, q] = (m_v[:, here] + mc_in[q, :, k * pw : (k + 1) * pw].astype(f32)).astype(bf16)
 
     grad = dot(cbuf[...].reshape(TOK, D), wd_v[...], NT)
+    mc_first.wait_recv()
+    chip_sum(0)
+    mx_first, mx_rest = [], []
+    for d in x_far:
+        other = lax.rem(x + d, NX)
+        mx_first.append(send(mx.at[other, 0], mx_in.at[x, 0], mx_s.at[0, d], mx_r.at[0, d], in_x(d)))
     a, u = gate_v[...].astype(f32), up_v[...].astype(f32)
     s = jax.nn.sigmoid(a)
     dg[...] = (grad * u * s * (1.0 + a * (1.0 - s))).astype(bf16)
     du[...] = (grad * (a * s)).astype(bf16)
+
+    def part_tile(j):
+        here = pl.ds(j * width, width)
+        value = dot(dg[...], wg_v[here, :], NT) + dot(du[...], wu_v[here, :], NT)
+        part[:, :, here] = value.astype(bf16).reshape(NY, rows, width)
+
+    tiles = D // width
+    for j in range(tiles // 2):
+        part_tile(j)
+
+    def give(k, src, to):
+        return send(src, ig_in.at[k], ig_s.at[k], ig_r.at[k], to)
+
     def total_of(ref, count):
         total = ref[0].astype(f32)
         for k in range(1, count):
             total = total + ref[k].astype(f32)
         return total
 
-    mc_copy.wait_recv()
-    for k in range(NX):
-        here = pl.ds(pl.multiple_of(core * hw + k * xw, xw), xw)
-        mx[k] = (m_v[:, here] + mc_in[:, k * xw : (k + 1) * xw].astype(f32)).astype(bf16)
-
     for copy in p1_copies:
         copy.wait_recv()
     p2_in[g] = total_of(p1_in, NZ)
     p2_copies = [send(p2_in.at[g], p2_in.at[g], p2_s.at[d], p2_r.at[d], in_group(d)) for d in g_far]
 
-    mx_copies = []
-    for d in x_far:
-        other = lax.rem(x + d, NX)
-        mx_copies.append(send(mx.at[other], mx_in.at[x], mx_s.at[d], mx_r.at[d], in_x(d)))
-
-    for j in range(D // width):
-        here = pl.ds(j * width, width)
-        value = dot(dg[...], wg_v[here, :], NT) + dot(du[...], wu_v[here, :], NT)
-        part[:, :, here] = value.astype(bf16).reshape(NY, rows, width)
-
-    def give(k, src, to):
-        return send(src, ig_in.at[k], ig_s.at[k], ig_r.at[k], to)
-
+    mc_rest.wait_recv()
+    for q in range(1, NQ):
+        chip_sum(q)
+    for j in range(tiles // 2, tiles):
+        part_tile(j)
     ig0 = give(0, part.at[y_opp, A], right)
     ig3 = give(3, part.at[y_opp, B], left)
     ig1 = give(1, part.at[y_right, B], right)
     ig4 = give(4, part.at[y_left, A], left)
-    mx_in[x] = mx[x]
-
     for copy in p2_copies:
         copy.wait_recv()
     t_v[z] = total_of(p2_in, G)
     p3_copies = [send(t_v.at[z], t_v.at[z], p3_s.at[d], p3_r.at[d], in_z(d)) for d in z_far]
+    for d in x_far:
+        other = lax.rem(x + d, NX)
+        src, dst = mx.at[other, rest], mx_in.at[x, rest]
+        mx_rest.append(send(src, dst, mx_s.at[1, d], mx_r.at[1, d], in_x(d)))
+    mx_in[x] = mx[x]
     for copy in p3_copies:
         copy.wait_recv()
 
@@ -231,9 +250,10 @@
     lax.fori_loop(0, RANK, column, 0)
     ts[...] = split(tt[...])
 
-    for copy in mx_copies:
+    for copy in mx_first + mx_rest:
         copy.wait_recv()
     m_sum = total_of(mx_in, NX)
+    m_sum = jnp.concatenate([m_sum[q] for q in range(NQ)], axis=1)
     m_high = m_sum.astype(bf16)
     m_low = (m_sum - m_high.astype(f32)).astype(bf16)
     r_all = fold(dot(ts[...], m_high)) + dot(ts[:RANK], m_low)
@@ -302,8 +322,9 @@
     RANK, F = tt.shape
     D = m_v.shape[1]
     hw = D // NC
-    xw = hw // NX
-    zw = xw // (NZ // 4)
+    qw = hw // NQ
+    pw = qw // NX
+    zw = NQ * pw // (NZ // 4)
     copies = [
         pltpu.make_async_copy(ig_v, ig, sems.at[0]),
         pltpu.make_async_copy(tt, left_out, sems.at[1]),
@@ -312,14 +333,14 @@
         copy.start()
     high = tt[...].astype(bf16).astype(f32)
     both = jnp.concatenate([high, tt[...] - high], axis=0).T.astype(bf16)
-    for k in range(NC * NX):
-        first = k * xw
+    for k in range(NC * NQ):
+        h, at = divmod(k % NQ * pw, zw)
         blocks = []
-        for h in range(NZ // 4):
-            rows = [rfull[k // NX, k % NX, 4 * h + q] for q in range(4)]
+        for chip in range(NX):
+            rows = [rfull[k // NQ, chip, 4 * h + q, :, at : at + pw] for q in range(4)]
             blocks.append(jnp.concatenate(rows, axis=0))
         block = jnp.concatenate(blocks, axis=1)
-        here = pl.ds(first, xw)
+        here = pl.ds(k * qw, qw)
         right_v[:, here] = block.astype(f32)
         update = dot(both, jnp.concatenate([block, block], axis=0))
         err_v[:, here] = (m_v[:, here] - update).astype(bf16)
@@ -339,8 +360,9 @@
     F = down_weight.shape[0]
     RANK = factor_in.shape[1]
     hw = D // NC
-    xw = hw // NX
-    zw = xw // (NZ // 4)
+    qw = hw // NQ
+    pw = qw // NX
+    zw = NQ * pw // (NZ // 4)
     VM = pltpu.VMEM
     DMA = pltpu.SemaphoreType.DMA
     piece = RANK // NZ
@@ -351,11 +373,11 @@
         VM((NY, rows, RANK), f32), VM((RANK, F), f32), VM((TOK, F), bf16), VM((TOK, F), bf16),
         VM((NY, rows, D), bf16), VM((6, half, D), bf16), VM((2, half, D), bf16),
         VM((NZ, piece, F), f32), VM((NZ, piece, F), f32), VM((G, piece, F), f32), VM((NZ, piece, F), f32),
-        VM((2 * RANK, F), bf16), VM((F, hw), bf16), VM((F, hw), bf16),
-        VM((NX, F, xw), bf16), VM((NX, F, xw), bf16), VM((NZ, 16, zw), bf16), VM((NZ, 16, zw), bf16),
+        VM((2 * RANK, F), bf16), VM((NQ, F, qw), bf16), VM((NQ, F, qw), bf16),
+        VM((NX, NQ, F, pw), bf16), VM((NX, NQ, F, pw), bf16), VM((NZ, 16, zw), bf16), VM((NZ, 16, zw), bf16),
         DMA((8,)), DMA((6,)), DMA((6,)),
         DMA((NZ,)), DMA((NZ,)), DMA((G,)), DMA((G,)), DMA((NZ,)), DMA((NZ,)),
-        DMA((1,)), DMA((1,)), DMA((NX,)), DMA((NX,)), DMA((NZ,)), DMA((NZ,)), DMA((NZ,)), DMA((NZ,)),
+        DMA((2,)), DMA((2,)), DMA((2, NX)), DMA((2, NX)), DMA((NZ,)), DMA((NZ,)), DMA((NZ,)), DMA((NZ,)),
         DMA((NX, NZ)), DMA((NX, NZ)), DMA((NX,)), DMA((NX,)), DMA((6,)), DMA((6,)),
     ]
     in_vmem = pl.BlockSpec(memory_space=pltpu.VMEM)
@@ -377,7 +399,7 @@
         out_shape=(shape((rows, D), bf16), shape((RANK, F), f32), shape((RANK, D), f32), shape((F, D), bf16)),
         in_specs=[in_vmem] * 4,
         out_specs=(anywhere,) * 4,
-        scratch_shapes=[VM((RANK, D), f32), VM((F, D), bf16), DMA((3 + NC * NX,))],
+        scratch_shapes=[VM((RANK, D), f32), VM((F, D), bf16), DMA((3 + NC * NQ,))],
         compiler_params=pltpu.CompilerParams(vmem_limit_bytes=16 * 1024 * 1024),
         cost_estimate=pl.CostEstimate(flops=3 * 10**8, bytes_accessed=9 * 10**6, transcendentals=0),
     )(*held)

time: 73.1 us -> 70.9 us (0.970)
  Pallas kernels: 72.4 us -> 70.2 us
    pallas_call x1, Pallas kernels: 70.4 us -> 68.2 us  [shards(): pl.pallas_call(kernel, out_shape=(VM((rows, D), bf16), VM((RANK, F), f32)...]
where the time goes in v4:
time: 70.9 us; the launch traced here: 70.8 us
  Pallas kernels  70.2 us (99%)
    pallas_call x1, Pallas kernels, shards(): pl.pallas_call(kernel, out_shape=(VM((rows, D), bf16), VM((RANK, F), f32)...  68.2 us
    pallas_call x1, Pallas kernels, shards(): pl.pallas_call(finish, out_shape=(shape((rows, D), bf16), shape((RANK, F)...  2.03 us

profile of v4, /device:TPU:1, one launch (start us, length us, event | category | flops | bytes accessed | tf_op | source)
XLA Modules:
  0.0 70.8 jit_solution(2754784668435450361)
XLA Ops:
  0.6 68.2 %shard_map.111 = (bf16[64,4096]{1,0:T(8,128)(2,1)S(1)}, f32[64,256]{1,0:T(8,128)S(1)}, bf16[2,4,8,16,256]{4,3,2,1,0:T(8,128)(2,1)S(1)}, f32[256,4096]{1,0:T(8,128)S(1)}) custom-call(bf16[64,4096]{1,0:T(8,128)(2,1)} %c.1, bf16[256,256]{1,0:T(8,128)(2,1)} %gate.1, bf16[256,256]{1,0:T(8,128)(2,1)} %up.1, bf16[256,4096]{1,0:T(8,128)(2,1)} %wd.1, ...), custom_call_target="tpu_custom_call" | custom-call | flops 4000000000 | bytes 17000000 | tf_op jit(solution)/shard_map/pallas_call | solution.py:385
  68.8 2.0 %shard_map.112 = (bf16[64,4096]{1,0:T(8,128)(2,1)}, f32[64,256]{1,0:T(8,128)}, f32[64,4096]{1,0:T(8,128)}, bf16[256,4096]{1,0:T(8,128)(2,1)}) custom-call(bf16[64,4096]{1,0:T(8,128)(2,1)S(1)} %get-tuple-element.12.ig_v, f32[64,256]{1,0:T(8,128)S(1)} %get-tuple-element.13.tt, bf16[2,4,8,16,256]{4,3,2,1,0:T(8,128)(2,1)S(1)} %get-tuple-element.14.rfull, ...), custom_call_target="tpu_custom_call" | custom-call | flops 300000000 | bytes 9000000 | tf_op jit(solution)/shard_map/pallas_call | solution.py:397

commit v5 on v4

--- a/solution.py
+++ b/solution.py
@@ -266,6 +266,13 @@
         r2_copies.append(send(r2.at[other], r2_in.at[z], r2_s.at[d], r2_r.at[d], in_z(d)))
     r2_in[z] = r2[z]
 
+    def all_left():
+        for copy in sent:
+            copy.wait_send()
+        sent.clear()
+
+    all_left()
+
     ig0.wait_recv()
     ig_sum[0] = (ig_in[0].astype(f32) + part[y_right, A].astype(f32)).astype(bf16)
     ig2 = give(2, ig_sum.at[0], right)
@@ -273,12 +280,6 @@
     ig_sum[1] = (ig_in[3].astype(f32) + part[y_left, B].astype(f32)).astype(bf16)
     ig5 = give(5, ig_sum.at[1], left)
 
-    def all_left():
-        for copy in sent:
-            copy.wait_send()
-        sent.clear()
-
-    all_left()
     for copy in r2_copies:
         copy.wait_recv()
     rfull[core, x, z] = (total_of(r2_in, NZ) * mean).astype(bf16)

time: 70.9 us -> 68.9 us (0.972)
  Pallas kernels: 70.2 us -> 68.2 us
    pallas_call x1, Pallas kernels: 68.2 us -> 66.2 us  [shards(): pl.pallas_call(kernel, out_shape=(VM((rows, D), bf16), VM((RANK, F), f32)...]
where the time goes in v5:
time: 68.9 us
  Pallas kernels  68.2 us (99%)
    pallas_call x1, Pallas kernels, shards(): pl.pallas_call(kernel, out_shape=(VM((rows, D), bf16), VM((RANK, F), f32)...  66.2 us
    pallas_call x1, Pallas kernels, shards(): pl.pallas_call(finish, out_shape=(shape((rows, D), bf16), shape((RANK, F)...  2.03 us

profile of v5, /device:TPU:1, one launch (start us, length us, event | category | flops | bytes accessed | tf_op | source)
XLA Modules:
  0.0 68.9 jit_solution(6794762723386613555)
XLA Ops:
  0.6 66.2 %shard_map.111 = (bf16[64,4096]{1,0:T(8,128)(2,1)S(1)}, f32[64,256]{1,0:T(8,128)S(1)}, bf16[2,4,8,16,256]{4,3,2,1,0:T(8,128)(2,1)S(1)}, f32[256,4096]{1,0:T(8,128)S(1)}) custom-call(bf16[64,4096]{1,0:T(8,128)(2,1)} %c.1, bf16[256,256]{1,0:T(8,128)(2,1)} %gate.1, bf16[256,256]{1,0:T(8,128)(2,1)} %up.1, bf16[256,4096]{1,0:T(8,128)(2,1)} %wd.1, ...), custom_call_target="tpu_custom_call" | custom-call | flops 4000000000 | bytes 17000000 | tf_op jit(solution)/shard_map/pallas_call | solution.py:386
  66.8 2.0 %shard_map.112 = (bf16[64,4096]{1,0:T(8,128)(2,1)}, f32[64,256]{1,0:T(8,128)}, f32[64,4096]{1,0:T(8,128)}, bf16[256,4096]{1,0:T(8,128)(2,1)}) custom-call(bf16[64,4096]{1,0:T(8,128)(2,1)S(1)} %get-tuple-element.12.ig_v, f32[64,256]{1,0:T(8,128)S(1)} %get-tuple-element.13.tt, bf16[2,4,8,16,256]{4,3,2,1,0:T(8,128)(2,1)S(1)} %get-tuple-element.14.rfull, ...), custom_call_target="tpu_custom_call" | custom-call | flops 300000000 | bytes 9000000 | tf_op jit(solution)/shard_map/pallas_call | solution.py:398

commit v6 on v5

--- a/solution.py
+++ b/solution.py
@@ -36,7 +36,7 @@
 def kernel(
     c, gate, up, wd, wg, wu, e, f,
     ig_v, tt, rfull, m_v,
-    cbuf, wd_v, wg_v, wu_v, e_v, f_v, fs, gate_v, up_v, hid, hid_t, y_v, pe, dg, du,
+    cbuf, wd_v, wg_v, wu_v, e_v, f_v, fs, gate_v, up_v, hid, hid_t, pe, dg, du,
     part, ig_in, ig_sum,
     p1, p1_in, p2_in, t_v, ts, mc, mc_in, mx, mx_in, r2, r2_in,
     load, ag_s, ag_r, p1_s, p1_r, p2_s, p2_r, p3_s, p3_r,
@@ -112,19 +112,8 @@
 
     loads[1].wait()
     fs[...] = split(f_v[...])
-    loads[0].wait()
-
-    def tokens_times_factor(slot):
-        both = dot(cbuf[slot], fs[...], NT)
-        y_v[slot] = both[:, :RANK] + both[:, RANK:]
-
-    tokens_times_factor(y)
     loads[2].wait()
     pe[...] = fold(dot(fs[...], e_v[...], NT))
-
-    from_left_b = gather(2, c.at[B], cbuf.at[y, B], right)
-    from_right_a = gather(3, c.at[A], cbuf.at[y, A], left)
-
     loads[3].wait()
     loads[4].wait()
     a, u = gate_v[...].astype(f32), up_v[...].astype(f32)
@@ -133,24 +122,30 @@
     hid[...] = hidden.astype(bf16)
     hid_t[...] = hidden.T.astype(bf16)
 
+    from_left_b = gather(2, c.at[B], cbuf.at[y, B], right)
+    from_right_a = gather(3, c.at[A], cbuf.at[y, A], left)
+
+    def left_of_block(slot):
+        block = fold(dot(fs[...], cbuf[slot], NT))
+        return fold(dot(split(block), hid[pl.ds(pl.multiple_of(slot * rows, rows), rows), :]))
+
+    loads[0].wait()
+    pe[...] += left_of_block(y)
+
     from_left_a.wait_recv()
     from_opp_a = gather(4, cbuf.at[y_left, A], cbuf.at[y_left, A], right)
     from_right_b.wait_recv()
     from_opp_b = gather(5, cbuf.at[y_right, B], cbuf.at[y_right, B], left)
     from_left_b.wait_recv()
-    tokens_times_factor(y_left)
+    pe[...] += left_of_block(y_left)
     from_right_a.wait_recv()
-    tokens_times_factor(y_right)
+    pe[...] += left_of_block(y_right)
     for k in (5, 6, 7):
         loads[k].wait()
     from_opp_a.wait_recv()
     from_opp_b.wait_recv()
-    tokens_times_factor(y_opp)
-
-    y_all = y_v[...].reshape(TOK, RANK)
-    y_high = y_all.astype(bf16).astype(f32)
-    y_both = jnp.concatenate([y_high, y_all - y_high], axis=1).T.astype(bf16)
-    p_all = fold(dot(y_both, hid[...])) + pe[...]
+    p_all = left_of_block(y_opp) + pe[...]
+
     p1[...] = p_all.reshape(NZ, RANK // NZ, F)
     p1_copies = []
     for d in z_far:
@@ -168,40 +163,22 @@
     rest = pl.ds(1, NQ - 1)
     mc[0] = weight_gradient((1 - core) * hw).astype(bf16)
     mc_first = send(mc.at[0], mc_in.at[0], mc_s.at[0], mc_r.at[0], sibling)
+    weight_gradient(core * hw)
     for q in range(1, NQ):
         mc[q] = weight_gradient((1 - core) * hw + q * qw).astype(bf16)
     mc_rest = send(mc.at[rest], mc_in.at[rest], mc_s.at[1], mc_r.at[1], sibling)
-    for q in range(NQ):
-        weight_gradient(core * hw + q * qw)
 
     def chip_sum(q):
         for k in range(NX):
             here = pl.ds(pl.multiple_of(core * hw + q * qw + k * pw, pw), pw)
             mx[k, q] = (m_v[:, here] + mc_in[q, :, k * pw : (k + 1) * pw].astype(f32)).astype(bf16)
 
-    grad = dot(cbuf[...].reshape(TOK, D), wd_v[...], NT)
     mc_first.wait_recv()
     chip_sum(0)
     mx_first, mx_rest = [], []
     for d in x_far:
         other = lax.rem(x + d, NX)
         mx_first.append(send(mx.at[other, 0], mx_in.at[x, 0], mx_s.at[0, d], mx_r.at[0, d], in_x(d)))
-    a, u = gate_v[...].astype(f32), up_v[...].astype(f32)
-    s = jax.nn.sigmoid(a)
-    dg[...] = (grad * u * s * (1.0 + a * (1.0 - s))).astype(bf16)
-    du[...] = (grad * (a * s)).astype(bf16)
-
-    def part_tile(j):
-        here = pl.ds(j * width, width)
-        value = dot(dg[...], wg_v[here, :], NT) + dot(du[...], wu_v[here, :], NT)
-        part[:, :, here] = value.astype(bf16).reshape(NY, rows, width)
-
-    tiles = D // width
-    for j in range(tiles // 2):
-        part_tile(j)
-
-    def give(k, src, to):
-        return send(src, ig_in.at[k], ig_s.at[k], ig_r.at[k], to)
 
     def total_of(ref, count):
         total = ref[0].astype(f32)
@@ -214,15 +191,18 @@
     p2_in[g] = total_of(p1_in, NZ)
     p2_copies = [send(p2_in.at[g], p2_in.at[g], p2_s.at[d], p2_r.at[d], in_group(d)) for d in g_far]
 
+    for q in range(1, NQ):
+        weight_gradient(core * hw + q * qw)
     mc_rest.wait_recv()
     for q in range(1, NQ):
         chip_sum(q)
-    for j in range(tiles // 2, tiles):
-        part_tile(j)
-    ig0 = give(0, part.at[y_opp, A], right)
-    ig3 = give(3, part.at[y_opp, B], left)
-    ig1 = give(1, part.at[y_right, B], right)
-    ig4 = give(4, part.at[y_left, A], left)
+
+    grad = dot(cbuf[...].reshape(TOK, D), wd_v[...], NT)
+    a, u = gate_v[...].astype(f32), up_v[...].astype(f32)
+    s = jax.nn.sigmoid(a)
+    dg[...] = (grad * u * s * (1.0 + a * (1.0 - s))).astype(bf16)
+    du[...] = (grad * (a * s)).astype(bf16)
+
     for copy in p2_copies:
         copy.wait_recv()
     t_v[z] = total_of(p2_in, G)
@@ -232,6 +212,22 @@
         src, dst = mx.at[other, rest], mx_in.at[x, rest]
         mx_rest.append(send(src, dst, mx_s.at[1, d], mx_r.at[1, d], in_x(d)))
     mx_in[x] = mx[x]
+
+    def part_tile(j):
+        here = pl.ds(j * width, width)
+        value = dot(dg[...], wg_v[here, :], NT) + dot(du[...], wu_v[here, :], NT)
+        part[:, :, here] = value.astype(bf16).reshape(NY, rows, width)
+
+    for j in range(D // width):
+        part_tile(j)
+
+    def give(k, src, to):
+        return send(src, ig_in.at[k], ig_s.at[k], ig_r.at[k], to)
+
+    ig0 = give(0, part.at[y_opp, A], right)
+    ig3 = give(3, part.at[y_opp, B], left)
+    ig1 = give(1, part.at[y_right, B], right)
+    ig4 = give(4, part.at[y_left, A], left)
     for copy in p3_copies:
         copy.wait_recv()
 
@@ -345,10 +341,10 @@
         right_v[:, here] = block.astype(f32)
         update = dot(both, jnp.concatenate([block, block], axis=0))
         err_v[:, here] = (m_v[:, here] - update).astype(bf16)
-        copies.append(pltpu.make_async_copy(err_v.at[:, here], err.at[:, here], sems.at[3 + k]))
+        copies.append(pltpu.make_async_copy(err_v.at[:, here], err.at[:, here], sems.at[2 + 2 * k]))
         copies[-1].start()
-    copies.append(pltpu.make_async_copy(right_v, right_out, sems.at[2]))
-    copies[-1].start()
+        copies.append(pltpu.make_async_copy(right_v.at[:, here], right_out.at[:, here], sems.at[3 + 2 * k]))
+        copies[-1].start()
     for copy in copies:
         copy.wait()
 
@@ -371,7 +367,7 @@
         VM((NY, rows, D), bf16), VM((F, D), bf16), VM((D, F), bf16), VM((D, F), bf16),
         VM((F, D), bf16), VM((RANK, D), f32), VM((2 * RANK, D), bf16),
         VM((TOK, F), bf16), VM((TOK, F), bf16), VM((TOK, F), bf16), VM((F, TOK), bf16),
-        VM((NY, rows, RANK), f32), VM((RANK, F), f32), VM((TOK, F), bf16), VM((TOK, F), bf16),
+        VM((RANK, F), f32), VM((TOK, F), bf16), VM((TOK, F), bf16),
         VM((NY, rows, D), bf16), VM((6, half, D), bf16), VM((2, half, D), bf16),
         VM((NZ, piece, F), f32), VM((NZ, piece, F), f32), VM((G, piece, F), f32), VM((NZ, piece, F), f32),
         VM((2 * RANK, F), bf16), VM((NQ, F, qw), bf16), VM((NQ, F, qw), bf16),
@@ -400,7 +396,7 @@
         out_shape=(shape((rows, D), bf16), shape((RANK, F), f32), shape((RANK, D), f32), shape((F, D), bf16)),
         in_specs=[in_vmem] * 4,
         out_specs=(anywhere,) * 4,
-        scratch_shapes=[VM((RANK, D), f32), VM((F, D), bf16), DMA((3 + NC * NQ,))],
+        scratch_shapes=[VM((RANK, D), f32), VM((F, D), bf16), DMA((2 + 2 * NC * NQ,))],
         compiler_params=pltpu.CompilerParams(vmem_limit_bytes=16 * 1024 * 1024),
         cost_estimate=pl.CostEstimate(flops=3 * 10**8, bytes_accessed=9 * 10**6, transcendentals=0),
     )(*held)

time: 68.9 us -> 68.9 us (level)
  no operation moved by 1% of the time
where the time goes in v6:
time: 68.9 us; the launch traced here: 68.8 us
  Pallas kernels  68.2 us (99%)
    pallas_call x1, Pallas kernels, shards(): pl.pallas_call(kernel, out_shape=(VM((rows, D), bf16), VM((RANK, F), f32)...  66.1 us
    pallas_call x1, Pallas kernels, shards(): pl.pallas_call(finish, out_shape=(shape((rows, D), bf16), shape((RANK, F)...  2.07 us

profile of v6, /device:TPU:1, one launch (start us, length us, event | category | flops | bytes accessed | tf_op | source)
XLA Modules:
  0.0 68.8 jit_solution(15690735187803977465)
XLA Ops:
  0.6 66.1 %shard_map.111 = (bf16[64,4096]{1,0:T(8,128)(2,1)S(1)}, f32[64,256]{1,0:T(8,128)S(1)}, bf16[2,4,8,16,256]{4,3,2,1,0:T(8,128)(2,1)S(1)}, f32[256,4096]{1,0:T(8,128)S(1)}) custom-call(bf16[64,4096]{1,0:T(8,128)(2,1)} %c.1, bf16[256,256]{1,0:T(8,128)(2,1)} %gate.1, bf16[256,256]{1,0:T(8,128)(2,1)} %up.1, bf16[256,4096]{1,0:T(8,128)(2,1)} %wd.1, ...), custom_call_target="tpu_custom_call" | custom-call | flops 4000000000 | bytes 17000000 | tf_op jit(solution)/shard_map/pallas_call | solution.py:382
  66.8 2.1 %shard_map.112 = (bf16[64,4096]{1,0:T(8,128)(2,1)}, f32[64,256]{1,0:T(8,128)}, f32[64,4096]{1,0:T(8,128)}, bf16[256,4096]{1,0:T(8,128)(2,1)}) custom-call(bf16[64,4096]{1,0:T(8,128)(2,1)S(1)} %get-tuple-element.12.ig_v, f32[64,256]{1,0:T(8,128)S(1)} %get-tuple-element.13.tt, bf16[2,4,8,16,256]{4,3,2,1,0:T(8,128)(2,1)S(1)} %get-tuple-element.14.rfull, ...), custom_call_target="tpu_custom_call" | custom-call | flops 300000000 | bytes 9000000 | tf_op jit(solution)/shard_map/pallas_call | solution.py:394

commit v7 on v6

--- a/solution.py
+++ b/solution.py
@@ -80,15 +80,14 @@
 
     mine = cbuf.at[y]
     pairs = [(c, mine), (f, f_v), (e, e_v), (gate, gate_v), (up, up_v), (wd, wd_v), (wg, wg_v), (wu, wu_v)]
+
+    barrier = pltpu.get_barrier_semaphore()
+    partners = [in_z(d) for d in z_far] + [in_group(d) for d in g_far] + [(dp, y_right), (dp, y_left)]
+    for other in partners:
+        pl.semaphore_signal(barrier, inc=1, device_id=other, device_id_type=MESH)
     loads = [pltpu.make_async_copy(a, b, load.at[k]) for k, (a, b) in enumerate(pairs)]
     for copy in loads:
         copy.start()
-
-    barrier = pltpu.get_barrier_semaphore()
-    partners = [(dp, y_right), (dp, y_left)]
-    partners += [in_group(d) for d in range(1, G)] + [in_z(d) for d in range(1, NZ)]
-    for other in partners:
-        pl.semaphore_signal(barrier, inc=1, device_id=other, device_id_type=MESH)
     pl.semaphore_wait(barrier, len(partners))
 
     sent = []

time: 68.9 us -> 68.6 us (level)
  no operation moved by 1% of the time
where the time goes in v7:
time: 68.6 us; the launch traced here: 68.5 us
  Pallas kernels  67.9 us (99%)
    pallas_call x1, Pallas kernels, shards(): pl.pallas_call(kernel, out_shape=(VM((rows, D), bf16), VM((RANK, F), f32)...  65.8 us
    pallas_call x1, Pallas kernels, shards(): pl.pallas_call(finish, out_shape=(shape((rows, D), bf16), shape((RANK, F)...  2.07 us

profile of v7, /device:TPU:1, one launch (start us, length us, event | category | flops | bytes accessed | tf_op | source)
XLA Modules:
  0.0 68.5 jit_solution(3513520077527943706)
XLA Ops:
  0.6 65.8 %shard_map.111 = (bf16[64,4096]{1,0:T(8,128)(2,1)S(1)}, f32[64,256]{1,0:T(8,128)S(1)}, bf16[2,4,8,16,256]{4,3,2,1,0:T(8,128)(2,1)S(1)}, f32[256,4096]{1,0:T(8,128)S(1)}) custom-call(bf16[64,4096]{1,0:T(8,128)(2,1)} %c.1, bf16[256,256]{1,0:T(8,128)(2,1)} %gate.1, bf16[256,256]{1,0:T(8,128)(2,1)} %up.1, bf16[256,4096]{1,0:T(8,128)(2,1)} %wd.1, ...), custom_call_target="tpu_custom_call" | custom-call | flops 4000000000 | bytes 17000000 | tf_op jit(solution)/shard_map/pallas_call | solution.py:381
  66.4 2.1 %shard_map.112 = (bf16[64,4096]{1,0:T(8,128)(2,1)}, f32[64,256]{1,0:T(8,128)}, f32[64,4096]{1,0:T(8,128)}, bf16[256,4096]{1,0:T(8,128)(2,1)}) custom-call(bf16[64,4096]{1,0:T(8,128)(2,1)S(1)} %get-tuple-element.12.ig_v, f32[64,256]{1,0:T(8,128)S(1)} %get-tuple-element.13.tt, bf16[2,4,8,16,256]{4,3,2,1,0:T(8,128)(2,1)S(1)} %get-tuple-element.14.rfull, ...), custom_call_target="tpu_custom_call" | custom-call | flops 300000000 | bytes 9000000 | tf_op jit(solution)/shard_map/pallas_call | solution.py:393

commit v8 on v7

--- a/solution.py
+++ b/solution.py
@@ -309,9 +309,13 @@
             r4_copies[d, k].wait_recv()
         came = rfull.at[core, lax.rem(x + NX - d, NX)]
         r5_copies.append(send(came, came, r5_s.at[d], r5_r.at[d], sibling))
+    for copy in sent:
+        if not any(copy is last for last in r5_copies):
+            copy.wait_send()
     for copy in r5_copies:
         copy.wait_recv()
-    all_left()
+    for copy in r5_copies:
+        copy.wait_send()
 
 
 def finish(ig_v, tt, rfull, m_v, ig, left_out, right_out, err, right_v, err_v, sems):

time: 68.6 us -> 68.5 us (level)
  no operation moved by 1% of the time
where the time goes in v8:
time: 68.5 us
  Pallas kernels  67.8 us (99%)
    pallas_call x1, Pallas kernels, shards(): pl.pallas_call(kernel, out_shape=(VM((rows, D), bf16), VM((RANK, F), f32)...  65.7 us
    pallas_call x1, Pallas kernels, shards(): pl.pallas_call(finish, out_shape=(shape((rows, D), bf16), shape((RANK, F)...  2.07 us

profile of v8, /device:TPU:1, one launch (start us, length us, event | category | flops | bytes accessed | tf_op | source)
XLA Modules:
  0.0 68.5 jit_solution(16532453350396024940)
XLA Ops:
  0.6 65.7 %shard_map.111 = (bf16[64,4096]{1,0:T(8,128)(2,1)S(1)}, f32[64,256]{1,0:T(8,128)S(1)}, bf16[2,4,8,16,256]{4,3,2,1,0:T(8,128)(2,1)S(1)}, f32[256,4096]{1,0:T(8,128)S(1)}) custom-call(bf16[64,4096]{1,0:T(8,128)(2,1)} %c.1, bf16[256,256]{1,0:T(8,128)(2,1)} %gate.1, bf16[256,256]{1,0:T(8,128)(2,1)} %up.1, bf16[256,4096]{1,0:T(8,128)(2,1)} %wd.1, ...), custom_call_target="tpu_custom_call" | custom-call | flops 4000000000 | bytes 17000000 | tf_op jit(solution)/shard_map/pallas_call | solution.py:385
  66.4 2.1 %shard_map.112 = (bf16[64,4096]{1,0:T(8,128)(2,1)}, f32[64,256]{1,0:T(8,128)}, f32[64,4096]{1,0:T(8,128)}, bf16[256,4096]{1,0:T(8,128)(2,1)}) custom-call(bf16[64,4096]{1,0:T(8,128)(2,1)S(1)} %get-tuple-element.12.ig_v, f32[64,256]{1,0:T(8,128)S(1)} %get-tuple-element.13.tt, bf16[2,4,8,16,256]{4,3,2,1,0:T(8,128)(2,1)S(1)} %get-tuple-element.14.rfull, ...), custom_call_target="tpu_custom_call" | custom-call | flops 300000000 | bytes 9000000 | tf_op jit(solution)/shard_map/pallas_call | solution.py:397
